TPU v7x, 1024 devices: a whole 4x4x32 slice. The times are simulated.
1024 devices in a mesh: dp: 64 (over z_lo, x, core), sub: 16 (over z_hi, y).
Axes of the slice: x: 4, y: 4, z: 32 (z_hi: 4, z_lo: 8; z = z_hi * 8 + z_lo), core: 2. Of those that a mesh axis runs over, the one named last changes fastest.
Arguments:
- queries: float32 [16384, 4096], P('dp', 'sub'), may hold values from -40 to 40
- passages: float32 [2048, 4096], P(('dp', 'sub')), may hold values from -40 to 40
- positive: int32 [16384], P('dp'), may hold values from 0 to 2047
- hard_negs: int32 [16384, 4], P('dp'), may hold values from 0 to 2047
Outputs:
- row_loss: float32 [16384], P('dp')
- query_grad: float32 [16384, 4096], P('dp', 'sub')
- passage_grad: float32 [2048, 4096], P(('dp', 'sub'))
All inputs are finite; a program needn't handle non-finite values.
Results may differ from a plain program's by a relative error of at most 0.015.
Values may be sent and summed in bfloat16 or wider, within the bound.
No kernel may reach another device: no remote copies, remote signals or barrier semaphores. Data moves between devices by JAX's collectives and lax.ppermute only.
A program may use at most 32 MiB of HBM per device.

v0:
```python
import math

import jax
import jax.numpy as jnp
from jax import lax
from jax.sharding import PartitionSpec as P

D = 4096


hard_weight = 4.0


def on_device(queries, passages, positive, hard_negs):
    logit_scale = 4.0 / math.sqrt(D)
    qfull = lax.all_gather(queries.astype(jnp.bfloat16), "sub", axis=1, tiled=True)
    pshare = lax.all_gather(passages.astype(jnp.bfloat16), "dp", axis=0, tiled=True)
    share_rows = pshare.shape[0]
    per_device = passages.shape[0]
    sub_count = lax.axis_size("sub")
    sub_index = lax.axis_index("sub")
    position = jnp.arange(share_rows, dtype=jnp.int32)
    column_ids = (
        position // per_device * sub_count + sub_index
    ) * per_device + position % per_device
    logits = logit_scale * lax.dot_general(
        qfull, pshare, (((1,), (1,)), ((), ())), preferred_element_type=jnp.float32
    )
    onehot = column_ids[None, :] == positive[:, None]
    hard_mask = jnp.any(hard_negs[:, :, None] == column_ids[None, None, :], axis=1)
    hard_mask = jnp.logical_and(hard_mask, jnp.logical_not(onehot))
    weight = jnp.where(hard_mask, jnp.float32(hard_weight), jnp.float32(1.0))
    local_pos = jnp.sum(jnp.where(onehot, logits, jnp.float32(0.0)), axis=1)
    rowmax = lax.pmax(jnp.max(logits, axis=1), "sub")
    scaled = weight * jnp.exp(logits - rowmax[:, None])
    totals, pos_logit = lax.psum((jnp.sum(scaled, axis=1), local_pos), "sub")
    row_loss = rowmax + jnp.log(totals) - pos_logit
    dscore = (logit_scale * (scaled / totals[:, None] - onehot.astype(jnp.float32))).astype(
        jnp.bfloat16
    )
    query_terms = jnp.dot(dscore, pshare, preferred_element_type=jnp.float32)
    query_grad = lax.psum_scatter(
        query_terms.astype(jnp.bfloat16), "sub", scatter_dimension=1, tiled=True
    ).astype(jnp.float32)
    passage_grad = lax.psum_scatter(
        lax.dot_general(
            dscore, qfull, (((0,), (0,)), ((), ())), preferred_element_type=jnp.float32
        ),
        "dp",
        scatter_dimension=0,
        tiled=True,
    )
    return (row_loss, query_grad, passage_grad)


def solution(mesh):
    placed = (P("dp", "sub"), P(("dp", "sub"), None), P("dp"), P("dp", None))
    return jax.shard_map(
        on_device,
        mesh=mesh,
        in_specs=placed,
        out_specs=(P("dp"), P("dp", "sub"), P(("dp", "sub"), None)),
        check_vma=False,
    )
```

profile of v0, /device:TPU:2, one launch (start us, length us, event | category | flops | bytes accessed | tf_op | source)
XLA Modules:
  0.0 1547.0 jit_solution(7304691068318792850)
XLA Ops:
  7.2 0.0 all-gather.6.cloned.1.call-start
  7.2 1.4 convert_bitcast_fusion
  8.6 0.0 all-gather.6.cloned.1.call-update
  8.6 0.0 all-gather.4.cloned.1.call-start
  8.7 1.6 convert_element_type.18
  10.3 0.0 all-reduce.4.cloned.1.call-start
  10.4 0.9 compare_reduce_fusion
  11.3 0.1 copy.9
  11.4 136.0 %all-gather.6.cloned.1.call-done = bf16[64,2,4096]{2,1,0:T(2,128)(2,1)} async-done(((bf16[1,2,4096]{2,1,0:T(2,128)(2,1)}), bf16[64,2,4096]{2,1,0:T(2,128)(2,1)}) %all-gather.6.cloned.1.call-update) | async-done | bytes 1048592 | tf_op jit(solution)/shard_map/all_gather | solution.py:17
  147.4 1.5 reshape.59
  148.9 178.8 %all-gather.4.cloned.1.call-done = bf16[256,4096]{1,0:T(8,128)(2,1)} async-done(((bf16[256,256]{1,0:T(8,128)(2,1)}), bf16[256,4096]{1,0:T(8,128)(2,1)}) %all-gather.4.cloned.1.call-update) | async-done | bytes 2097168 | tf_op jit(solution)/shard_map/all_gather | solution.py:16
  327.7 2.6 fusion.13
  330.2 71.8 %pmax.7 = f32[256]{0:T(256)S(1)} all-reduce(f32[256]{0:T(256)S(1)} %get-tuple-element.7), channel_id=1, replica_groups=mesh['dp'=64,'sub'=16] {'sub'}, use_global_device_ids=true, to_apply=%region_1.2 | all-reduce | flops 256 | bytes 2048 | tf_op jit(solution)/shard_map/pmax | solution.py:34
  402.0 0.1 fusion.5
  402.2 65.5 %all-reduce.1 = (f32[256]{0:T(256)S(1)}, f32[256]{0:T(256)S(1)}) all-reduce(f32[256]{0:T(256)S(1)} %get-tuple-element.4, f32[256]{0:T(256)S(1)} %get-tuple-element.3), channel_id=1, replica_groups=mesh['dp'=64,'sub'=16] {'sub'}, use_global_device_ids=true, to_apply=%region_6.7 | all-reduce | flops 512 | bytes 4096 | tf_op jit(solution)/shard_map/psum | solution.py:36
  467.7 1.9 fusion.10
  469.6 0.0 reduce-scatter.2.cloned.1.call-start
  469.6 2.1 convolution_convert_fusion
  471.8 1.3 dynamic-slice
  473.7 0.6 add_subtract_fusion
  474.3 840.8 %all-reduce.4.cloned.1.call-done = f32[128,4096]{1,0:T(8,128)} async-done(((f32[128,4096]{1,0:T(8,128)}), f32[128,4096]{1,0:T(8,128)}) %all-reduce.4.cloned.1.call-update) | async-done | bytes 2097168
  1315.1 1.5 constant_dynamic-slice_fusion
  1316.6 222.2 %reduce-scatter.2.cloned.1.call-done = bf16[256,256]{1,0:T(8,128)(2,1)} async-done(((bf16[256,4096]{1,0:T(8,128)(2,1)}), bf16[256,256]{1,0:T(8,128)(2,1)}) %reduce-scatter.2.cloned.1.call-update) | async-done | bytes 131088 | tf_op jit(solution)/shard_map/reduce_scatter | solution.py:42
  1538.8 1.6 convert_element_type.23
  (8 shorter events, 0.1 us)
Async XLA Ops:
  7.2 140.2 %all-gather.6.cloned.1.call-start = ((), (), s32[]{:S(2)}) async-start(), calls=%async_computation.3 | async-start | bytes 1064960 | tf_op jit(solution)/shard_map/all_gather | solution.py:17
  8.6 319.0 %all-gather.4.cloned.1.call-start = ((), (), s32[]{:S(2)}) async-start(), calls=%async_computation.1 | async-start | bytes 2228224 | tf_op jit(solution)/shard_map/all_gather | solution.py:16
  10.3 1304.8 %all-reduce.4.cloned.1.call-start = ((), (), s32[]{:S(2)}) async-start(), calls=%async_computation.4 | async-start | bytes 4194304
  148.9 253.1 %copy-start.1 = (s32[256]{0:T(256)S(1)}, s32[256]{0:T(256)}, u32[]{:S(2)}) copy-start(s32[256]{0:T(256)} %param.6) | copy-start | bytes 3076
  327.7 140.0 %copy-start = (bf16[256,4096]{1,0:T(8,128)(2,1)S(1)}, bf16[256,4096]{1,0:T(8,128)(2,1)}, u32[]{:S(2)}) copy-start(bf16[256,4096]{1,0:T(8,128)(2,1)} %all-gather.4.cloned.1.call-done) | copy-start | bytes 6291460
  469.6 1069.3 %reduce-scatter.2.cloned.1.call-start = ((), (), s32[]{:S(2)}) async-start(), calls=%async_computation.2 | async-start | bytes 2228224 | tf_op jit(solution)/shard_map/reduce_scatter | solution.py:42
Sparse Core Ops, SparseCore 0:
  11.3 136.0 all-gather.5
  152.1 175.4 all-gather.3
  469.7 845.3 all-reduce.3
  1321.1 217.7 reduce-scatter.1
where the time goes:
time: 1550 us
  waiting for transfers between devices  1380 us (89%)
  blocking collectives  137 us (9%)
    unnamed x5, waiting for transfers between devices  841 us
    reduce_scatter x1, waiting for transfers between devices, on_device(): lax.psum_scatter(query_terms.astype(jnp.bfloat16), 'sub', scatter_dimensi...  222 us
    all_gather x1, waiting for transfers between devices, on_device(): lax.all_gather(queries.astype(jnp.bfloat16), 'sub', axis=1, tiled=True)  179 us
    all_gather x1, waiting for transfers between devices, on_device(): lax.all_gather(passages.astype(jnp.bfloat16), 'dp', axis=0, tiled=True)  136 us
    pmax x1, blocking collectives, on_device(): rowmax = lax.pmax(jnp.max(logits, axis=1), 'sub')  71.8 us
    psum x1, blocking collectives, on_device(): totals, pos_logit = lax.psum((jnp.sum(scaled, axis=1), local_pos), 'sub')  65.5 us
  transfers between devices with their start and end apart: 4, of which 4 were waited for; matrix products, arithmetic and copies ran while one was open for 1% of the time, Pallas kernels for 0%

commit v1 on v0

v1 whole, which is shorter than its diff:
```python
import math

import jax
import jax.numpy as jnp
from jax import lax
from jax.experimental import pallas as pl
from jax.experimental.pallas import tpu as pltpu
from jax.sharding import Mesh, PartitionSpec as P

D = 4096
ZL, X, C, ZH, Y = 8, 4, 2, 4, 4
PLANE = ("x", "c", "y")
XC = ("x", "c")
SUB = ("zh", "y")
G = X * C
hard_weight = 4.0
logit_scale = 4.0 / math.sqrt(D)
bf16, f32 = jnp.bfloat16, jnp.float32
params = pltpu.CompilerParams(vmem_limit_bytes=40 * 2**20)


def exchange(x, axes):
    return lax.all_to_all(x, axes, 0, 0, tiled=True)


def assemble(q_ref, rows_ref):
    groups, parts, n, k = q_ref.shape
    for g in range(groups):
        for s in range(parts):
            rows_ref[g * n : (g + 1) * n, s * k : (s + 1) * k] = q_ref[g, s]


def logits_kernel(q_ref, p_ref, out_ref, rows_ref):
    assemble(q_ref, rows_ref)
    out_ref[...] = lax.dot_general(
        rows_ref[...], p_ref[...], (((1,), (1,)), ((), ())), preferred_element_type=f32
    )


def softmax_kernel(part_ref, ids_ref, ds_ref, loss_ref):
    rows, n = part_ref.shape[1:]
    positive = ids_ref[:, 0:1]
    col = lax.broadcasted_iota(jnp.int32, (rows, n), 1)
    base = (col >> 5) * (G * 32) + (col & 31)
    logits, top = [], None
    for g in range(G):
        a = part_ref[g * Y]
        for y in range(1, Y):
            a = a + part_ref[g * Y + y]
        a = a * logit_scale
        logits.append(a)
        m = jnp.max(a, axis=1, keepdims=True)
        top = m if top is None else jnp.maximum(top, m)
    total = jnp.zeros((rows, 1), f32)
    pos_logit = jnp.zeros((rows, 1), f32)
    scaled, hot = [], []
    for g in range(G):
        ids = base + g * 32
        onehot = ids == positive
        hard = ids == ids_ref[:, 1:2]
        for h in range(2, ids_ref.shape[1]):
            hard = jnp.logical_or(hard, ids == ids_ref[:, h : h + 1])
        hard = jnp.logical_and(hard, jnp.logical_not(onehot))
        e = jnp.where(hard, hard_weight, 1.0) * jnp.exp(logits[g] - top)
        total = total + jnp.sum(e, axis=1, keepdims=True)
        pos_logit = pos_logit + jnp.sum(jnp.where(onehot, logits[g], 0.0), axis=1, keepdims=True)
        scaled.append(e)
        hot.append(jnp.where(onehot, 1.0, 0.0))
    loss_ref[...] = top + jnp.log(total) - pos_logit
    for g in range(G):
        ds = (logit_scale * (scaled[g] / total - hot[g])).astype(bf16)
        for y in range(Y):
            ds_ref[g * Y + y] = ds


def grads_kernel(ds_ref, q_ref, p_ref, qg_ref, pg_ref, rows_ref):
    groups, parts, n, k = q_ref.shape
    assemble(q_ref, rows_ref)
    for g in range(groups):
        terms = jnp.dot(ds_ref[g * n : (g + 1) * n, :], p_ref[...], preferred_element_type=f32)
        for s in range(parts):
            qg_ref[g, s] = terms[:, s * k : (s + 1) * k].astype(bf16)
    pg_ref[...] = lax.dot_general(
        ds_ref[...], rows_ref[...], (((0,), (0,)), ((), ())), preferred_element_type=f32
    ).astype(bf16)


def on_device(queries, passages, positive, hard_negs):
    nq, k = queries.shape
    own = passages.shape[0]
    nz = nq // ZH
    nrow = nz // Y
    width = ZH * k
    sub = lax.axis_index(SUB)

    p = passages.astype(bf16).reshape(own, ZH, Y, k).transpose(2, 0, 1, 3).reshape(Y, own, width)
    p = jnp.broadcast_to(p[None], (ZH, Y, own, width)).reshape(ZH * Y, own, width)
    p = exchange(p, SUB).reshape(ZH * Y * own, width)
    p = jnp.broadcast_to(p[None], (ZL,) + p.shape)
    p = exchange(p, "zl").reshape(ZL * ZH * Y * own, width)

    q = exchange(queries.astype(bf16).reshape(ZH, nz, k), "zh")
    q = exchange(jnp.broadcast_to(q[None], (G,) + q.shape), XC)

    np_ = p.shape[0]
    parts = pl.pallas_call(
        logits_kernel,
        out_shape=jax.ShapeDtypeStruct((G * nz, np_), f32),
        scratch_shapes=[pltpu.VMEM((G * nz, width), bf16)],
        compiler_params=params,
        name="logits",
    )(q, p)
    parts = exchange(parts.reshape(G * Y, nrow, np_), PLANE)

    ids = jnp.concatenate([positive[:, None], hard_negs], axis=1)
    ids = lax.dynamic_slice_in_dim(ids, sub * nrow, nrow, 0)
    ds, loss = pl.pallas_call(
        softmax_kernel,
        out_shape=(
            jax.ShapeDtypeStruct((G * Y, nrow, np_), bf16),
            jax.ShapeDtypeStruct((nrow, 1), f32),
        ),
        compiler_params=params,
        name="softmax",
    )(parts, ids)
    row_loss = exchange(jnp.broadcast_to(loss.reshape(1, nrow), (ZH * Y, nrow)), SUB).reshape(nq)
    ds = exchange(ds, PLANE).reshape(G * nz, np_)

    qg, pg = pl.pallas_call(
        grads_kernel,
        out_shape=(
            jax.ShapeDtypeStruct(q.shape, bf16),
            jax.ShapeDtypeStruct((np_, width), bf16),
        ),
        scratch_shapes=[pltpu.VMEM((G * nz, width), bf16)],
        compiler_params=params,
        name="grads",
    )(ds, q, p)

    pg = exchange(pg.reshape(ZL, np_ // ZL, width), "zl")
    pg = jnp.sum(pg.astype(f32), axis=0).astype(bf16)
    pg = exchange(pg.reshape(ZH * Y, own, width), SUB)
    pg = jnp.sum(pg.astype(f32).reshape(ZH, Y, own, width), axis=0)
    pg = pg.reshape(Y, own, ZH, k).transpose(1, 2, 0, 3).reshape(own, ZH * Y * k)

    qg = jnp.sum(exchange(qg, XC).astype(f32), axis=0).astype(bf16)
    qg = exchange(qg, "zh").reshape(nq, k).astype(f32)
    return row_loss, qg, pg


def solution(mesh):
    fine = Mesh(mesh.devices.reshape(ZL, X, C, ZH, Y), ("zl", "x", "c", "zh", "y"))
    dp, sub = ("zl", "x", "c"), ("zh", "y")
    return jax.shard_map(
        on_device,
        mesh=fine,
        in_specs=(P(dp, sub), P(dp + sub, None), P(dp), P(dp, None)),
        out_specs=(P(dp), P(dp, sub), P(dp + sub, None)),
        check_vma=False,
    )
```

time: 1550 us -> 317 us (0.20)
  waiting for transfers between devices: 1380 us -> 151 us
  starting transfers between devices: 0.16 us -> 68.8 us
  blocking collectives: 137 us -> 82 us
    unnamed x5 -> x0, waiting for transfers between devices: 841 us -> none
    all_gather x2 -> x0, waiting for transfers between devices: 315 us -> none  [the longest x1 179 us: on_device(): lax.all_gather(queries.astype(jnp.bfloat16), 'sub', axis=1, tiled=True)]
    reduce_scatter x1 -> x0, waiting for transfers between devices: 222 us -> none  [on_device(): lax.psum_scatter(query_terms.astype(jnp.bfloat16), 'sub', scatter_dimensi...]
    all_to_all x0 -> x8, waiting for transfers between devices: none -> 151 us  [exchange(): return lax.all_to_all(x, axes, 0, 0, tiled=True)]
    all_to_all x0 -> x3, blocking collectives: none -> 82 us  [exchange(): return lax.all_to_all(x, axes, 0, 0, tiled=True)]
    pmax x1 -> x0, blocking collectives: 71.8 us -> none  [on_device(): rowmax = lax.pmax(jnp.max(logits, axis=1), 'sub')]
    all_to_all x0 -> x8, starting transfers between devices: none -> 68.8 us  [exchange(): return lax.all_to_all(x, axes, 0, 0, tiled=True)]
    psum x1 -> x0, blocking collectives: 65.5 us -> none  [on_device(): totals, pos_logit = lax.psum((jnp.sum(scaled, axis=1), local_pos), 'sub')]
  transfers between devices with their start and end apart: 4 -> 8, of which waited for: 4 -> 8; matrix products, arithmetic and copies ran while one was open for 1% -> 1% of each run, Pallas kernels for 0% -> 1%
where the time goes in v1:
time: 317 us; the launch traced here: 316 us
  waiting for transfers between devices  151 us (48%)
  blocking collectives  82 us (26%)
  starting transfers between devices  68.8 us (22%)
  local copies, waits for them, and re-layouts  5.77 us (2%)
  Pallas kernels  4.24 us (1%)
  other arithmetic  3.38 us (1%)
    all_to_all x8, waiting for transfers between devices, exchange(): return lax.all_to_all(x, axes, 0, 0, tiled=True)  151 us
    all_to_all x3, blocking collectives, exchange(): return lax.all_to_all(x, axes, 0, 0, tiled=True)  82 us
    all_to_all x8, starting transfers between devices, exchange(): return lax.all_to_all(x, axes, 0, 0, tiled=True)  68.8 us
  transfers between devices with their start and end apart: 8, of which 8 were waited for; matrix products, arithmetic and copies ran while one was open for 1% of the time, Pallas kernels for 1%

profile of v1, /device:TPU:2, one launch (start us, length us, event | category | flops | bytes accessed | tf_op | source)
XLA Modules:
  0.0 316.1 jit_solution(10795612757856659933)
XLA Ops:
  2.2 31.1 %all-to-all-start.2 = ((bf16[16,2,1024]{2,1,0:T(2,128)(2,1)}), bf16[16,2,1024]{2,1,0:T(2,128)(2,1)S(1)}, u32[]{:S(2)}, u32[]{:S(2)}) async-start(bf16[16,2,1024]{2,1,0:T(2,128)(2,1)} %bitcast.2), calls=%async_computation.2 | async-start | bytes 131072 | tf_op jit(solution)/shard_map/all_to_all | solution.py:23
  33.3 24.5 %all-to-all-done.2 = bf16[16,2,1024]{2,1,0:T(2,128)(2,1)S(1)} async-done(((bf16[16,2,1024]{2,1,0:T(2,128)(2,1)}), bf16[16,2,1024]{2,1,0:T(2,128)(2,1)S(1)}, u32[]{:S(2)}, u32[]{:S(2)}) %all-to-all-start.2) | async-done | bytes 65568 | tf_op jit(solution)/shard_map/all_to_all | solution.py:23
  57.8 29.8 %all_to_all.56 = bf16[4,64,256]{2,1,0:T(8,128)(2,1)S(1)} all-to-all(bf16[4,64,256]{2,1,0:T(8,128)(2,1)S(1)} %bitcast.21), channel_id=1, replica_groups=mesh['zl'=8,'x'=4,'c'=2,'zh'=4,'y'=4] {'zh'}, dimensions={0} | all-to-all | bytes 262144 | tf_op jit(solution)/shard_map/all_to_all | solution.py:23
  87.5 1.1 broadcast_in_dim.30
  88.6 4.8 %all-to-all-start.1 = ((bf16[8,4,64,256]{3,2,1,0:T(8,128)(2,1)}), bf16[8,4,64,256]{3,2,1,0:T(8,128)(2,1)S(1)}, u32[]{:S(2)}, u32[]{:S(2)}) async-start(bf16[8,4,64,256]{3,2,1,0:T(8,128)(2,1)} %broadcast_in_dim.30), calls=%async_computation.1 | async-start | bytes 2097152 | tf_op jit(solution)/shard_map/all_to_all | solution.py:23
  93.5 14.5 %all-to-all-done.1.q_ref = bf16[8,4,64,256]{3,2,1,0:T(8,128)(2,1)S(1)} async-done(((bf16[8,4,64,256]{3,2,1,0:T(8,128)(2,1)}), bf16[8,4,64,256]{3,2,1,0:T(8,128)(2,1)S(1)}, u32[]{:S(2)}, u32[]{:S(2)}) %all-to-all-start.1) | async-done | bytes 1048608 | tf_op jit(solution)/shard_map/all_to_all | solution.py:23
  108.0 33.8 %all_to_all.57 = bf16[8,32,1024]{2,1,0:T(8,128)(2,1)S(1)} all-to-all(bf16[8,32,1024]{2,1,0:T(8,128)(2,1)S(1)} %broadcast_in_dim.34), channel_id=1, replica_groups=mesh['zl'=8,'x'=4,'c'=2,'zh'=4,'y'=4] {'zl'}, dimensions={0} | all-to-all | bytes 1048576 | tf_op jit(solution)/shard_map/all_to_all | solution.py:23
  141.8 1.3 logits.1
  143.1 6.4 %all-to-all-start.4 = ((f32[32,16,256]{2,1,0:T(8,128)}), f32[32,16,256]{2,1,0:T(8,128)S(1)}, u32[]{:S(2)}, u32[]{:S(2)}) async-start(f32[32,16,256]{2,1,0:T(8,128)} %bitcast.4), calls=%async_computation.4 | async-start | bytes 1048576 | tf_op jit(solution)/shard_map/all_to_all | solution.py:23
  150.3 9.5 %all-to-all-done.4.part_ref = f32[32,16,256]{2,1,0:T(8,128)S(1)} async-done(((f32[32,16,256]{2,1,0:T(8,128)}), f32[32,16,256]{2,1,0:T(8,128)S(1)}, u32[]{:S(2)}, u32[]{:S(2)}) %all-to-all-start.4) | async-done | bytes 524320 | tf_op jit(solution)/shard_map/all_to_all | solution.py:23
  159.8 1.0 softmax.1
  160.8 5.2 %all-to-all-start.6 = ((bf16[32,16,256]{2,1,0:T(8,128)(2,1)}), bf16[32,16,256]{2,1,0:T(8,128)(2,1)S(1)}, u32[]{:S(2)}, u32[]{:S(2)}) async-start(bf16[32,16,256]{2,1,0:T(8,128)(2,1)} %get-tuple-element.8), calls=%async_computation.6 | async-start | bytes 524288 | tf_op jit(solution)/shard_map/all_to_all | solution.py:23
  166.2 7.8 %all-to-all-done.6 = bf16[32,16,256]{2,1,0:T(8,128)(2,1)S(1)} async-done(((bf16[32,16,256]{2,1,0:T(8,128)(2,1)}), bf16[32,16,256]{2,1,0:T(8,128)(2,1)S(1)}, u32[]{:S(2)}, u32[]{:S(2)}) %all-to-all-start.6) | async-done | bytes 262176 | tf_op jit(solution)/shard_map/all_to_all | solution.py:23
  174.6 5.3 %all-to-all-start.5 = ((f32[16,1,16]{2,1,0:T(1,128)}), f32[16,1,16]{2,1,0:T(1,128)S(1)}, u32[]{:S(2)}, u32[]{:S(2)}) async-start(f32[16,1,16]{2,1,0:T(1,128)} %broadcast_in_dim.37), calls=%async_computation.5 | async-start | bytes 16384 | tf_op jit(solution)/shard_map/all_to_all | solution.py:23
  179.9 2.0 grads.1
  181.9 22.3 %all-to-all-done.5 = f32[16,1,16]{2,1,0:T(1,128)S(1)} async-done(((f32[16,1,16]{2,1,0:T(1,128)}), f32[16,1,16]{2,1,0:T(1,128)S(1)}, u32[]{:S(2)}, u32[]{:S(2)}) %all-to-all-start.5) | async-done | bytes 1056 | tf_op jit(solution)/shard_map/all_to_all | solution.py:23
  204.2 18.4 %all_to_all.58 = bf16[8,4,64,256]{3,2,1,0:T(8,128)(2,1)S(1)} all-to-all(bf16[8,4,64,256]{3,2,1,0:T(8,128)(2,1)S(1)} %get-tuple-element.9), channel_id=1, replica_groups=mesh['zl'=8,'x'=4,'c'=2,'zh'=4,'y'=4] {'x','c'}, dimensions={0} | all-to-all | bytes 2097152 | tf_op jit(solution)/shard_map/all_to_all | solution.py:23
  222.6 4.3 %all-to-all-start.9 = ((bf16[8,32,1024]{2,1,0:T(8,128)(2,1)}), bf16[8,32,1024]{2,1,0:T(8,128)(2,1)S(1)}, u32[]{:S(2)}, u32[]{:S(2)}) async-start(bf16[8,32,1024]{2,1,0:T(8,128)(2,1)} %bitcast.8), calls=%async_computation.9 | async-start | bytes 1048576 | tf_op jit(solution)/shard_map/all_to_all | solution.py:23
  226.9 0.8 reduce_sum.33
  227.7 27.5 %all-to-all-done.9 = bf16[8,32,1024]{2,1,0:T(8,128)(2,1)S(1)} async-done(((bf16[8,32,1024]{2,1,0:T(8,128)(2,1)}), bf16[8,32,1024]{2,1,0:T(8,128)(2,1)S(1)}, u32[]{:S(2)}, u32[]{:S(2)}) %all-to-all-start.9) | async-done | bytes 524320 | tf_op jit(solution)/shard_map/all_to_all | solution.py:23
  255.2 3.3 %all-to-all-start.8 = ((bf16[4,64,256]{2,1,0:T(8,128)(2,1)}), bf16[4,64,256]{2,1,0:T(8,128)(2,1)S(1)}, u32[]{:S(2)}, u32[]{:S(2)}) async-start(bf16[4,64,256]{2,1,0:T(8,128)(2,1)} %reduce_sum.33), calls=%async_computation.8 | async-start | bytes 262144 | tf_op jit(solution)/shard_map/all_to_all | solution.py:23
  259.3 23.0 %all-to-all-done.8 = bf16[4,64,256]{2,1,0:T(8,128)(2,1)S(1)} async-done(((bf16[4,64,256]{2,1,0:T(8,128)(2,1)}), bf16[4,64,256]{2,1,0:T(8,128)(2,1)S(1)}, u32[]{:S(2)}, u32[]{:S(2)}) %all-to-all-start.8) | async-done | bytes 131104 | tf_op jit(solution)/shard_map/all_to_all | solution.py:23
  282.3 8.5 %all-to-all-start.10 = ((bf16[16,2,1024]{2,1,0:T(2,128)(2,1)}), bf16[16,2,1024]{2,1,0:T(2,128)(2,1)S(1)}, u32[]{:S(2)}, u32[]{:S(2)}) async-start(bf16[16,2,1024]{2,1,0:T(2,128)(2,1)} %reshape.69), calls=%async_computation.10 | async-start | bytes 131072 | tf_op jit(solution)/shard_map/all_to_all | solution.py:23
  293.4 21.9 %all-to-all-done.10 = bf16[16,2,1024]{2,1,0:T(2,128)(2,1)S(1)} async-done(((bf16[16,2,1024]{2,1,0:T(2,128)(2,1)}), bf16[16,2,1024]{2,1,0:T(2,128)(2,1)S(1)}, u32[]{:S(2)}, u32[]{:S(2)}) %all-to-all-start.10) | async-done | bytes 65568 | tf_op jit(solution)/shard_map/all_to_all | solution.py:23
  (28 shorter events, 7.2 us)
Async XLA Ops:
  0.6 32.6 %copy-start = (f32[256,256]{1,0:T(8,128)S(1)}, f32[256,256]{1,0:T(8,128)}, u32[]{:S(2)}) copy-start(f32[256,256]{1,0:T(8,128)} %param.4) | copy-start | bytes 786436
  2.2 55.6 %all-to-all-start.2 = ((bf16[16,2,1024]{2,1,0:T(2,128)(2,1)}), bf16[16,2,1024]{2,1,0:T(2,128)(2,1)S(1)}, u32[]{:S(2)}, u32[]{:S(2)}) async-start(bf16[16,2,1024]{2,1,0:T(2,128)(2,1)} %bitcast.2), calls=%async_computation.2 | async-start | bytes 131072 | tf_op jit(solution)/shard_map/all_to_all | solution.py:23
  88.6 19.3 %all-to-all-start.1 = ((bf16[8,4,64,256]{3,2,1,0:T(8,128)(2,1)}), bf16[8,4,64,256]{3,2,1,0:T(8,128)(2,1)S(1)}, u32[]{:S(2)}, u32[]{:S(2)}) async-start(bf16[8,4,64,256]{3,2,1,0:T(8,128)(2,1)} %broadcast_in_dim.30), calls=%async_computation.1 | async-start | bytes 2097152 | tf_op jit(solution)/shard_map/all_to_all | solution.py:23
  143.1 16.7 %all-to-all-start.4 = ((f32[32,16,256]{2,1,0:T(8,128)}), f32[32,16,256]{2,1,0:T(8,128)S(1)}, u32[]{:S(2)}, u32[]{:S(2)}) async-start(f32[32,16,256]{2,1,0:T(8,128)} %bitcast.4), calls=%async_computation.4 | async-start | bytes 1048576 | tf_op jit(solution)/shard_map/all_to_all | solution.py:23
  149.5 0.7 copy-start.1
  149.5 0.7 copy-start.2
  160.8 13.2 %all-to-all-start.6 = ((bf16[32,16,256]{2,1,0:T(8,128)(2,1)}), bf16[32,16,256]{2,1,0:T(8,128)(2,1)S(1)}, u32[]{:S(2)}, u32[]{:S(2)}) async-start(bf16[32,16,256]{2,1,0:T(8,128)(2,1)} %get-tuple-element.8), calls=%async_computation.6 | async-start | bytes 524288 | tf_op jit(solution)/shard_map/all_to_all | solution.py:23
  174.6 29.6 %all-to-all-start.5 = ((f32[16,1,16]{2,1,0:T(1,128)}), f32[16,1,16]{2,1,0:T(1,128)S(1)}, u32[]{:S(2)}, u32[]{:S(2)}) async-start(f32[16,1,16]{2,1,0:T(1,128)} %broadcast_in_dim.37), calls=%async_computation.5 | async-start | bytes 16384 | tf_op jit(solution)/shard_map/all_to_all | solution.py:23
  222.6 32.6 %all-to-all-start.9 = ((bf16[8,32,1024]{2,1,0:T(8,128)(2,1)}), bf16[8,32,1024]{2,1,0:T(8,128)(2,1)S(1)}, u32[]{:S(2)}, u32[]{:S(2)}) async-start(bf16[8,32,1024]{2,1,0:T(8,128)(2,1)} %bitcast.8), calls=%async_computation.9 | async-start | bytes 1048576 | tf_op jit(solution)/shard_map/all_to_all | solution.py:23
  255.2 27.1 %all-to-all-start.8 = ((bf16[4,64,256]{2,1,0:T(8,128)(2,1)}), bf16[4,64,256]{2,1,0:T(8,128)(2,1)S(1)}, u32[]{:S(2)}, u32[]{:S(2)}) async-start(bf16[4,64,256]{2,1,0:T(8,128)(2,1)} %reduce_sum.33), calls=%async_computation.8 | async-start | bytes 262144 | tf_op jit(solution)/shard_map/all_to_all | solution.py:23
  282.3 33.0 %all-to-all-start.10 = ((bf16[16,2,1024]{2,1,0:T(2,128)(2,1)}), bf16[16,2,1024]{2,1,0:T(2,128)(2,1)S(1)}, u32[]{:S(2)}, u32[]{:S(2)}) async-start(bf16[16,2,1024]{2,1,0:T(2,128)(2,1)} %reshape.69), calls=%async_computation.10 | async-start | bytes 131072 | tf_op jit(solution)/shard_map/all_to_all | solution.py:23

commit v2 on v1

v2 whole, which is shorter than its diff:
```python
import math

import jax
import jax.numpy as jnp
from jax import lax
from jax.experimental import pallas as pl
from jax.experimental.pallas import tpu as pltpu
from jax.sharding import Mesh, PartitionSpec as P

D = 4096
SIZES = {"za": 2, "zb": 4, "x": 4, "c": 2, "zh": 4, "y": 4}
ZA, ZB, X, C, ZH, Y = SIZES.values()
FAR = ("za", "zh")
NEAR = ("zb", "y")
PLANE = ("x", "c", "y")
G = X * C
A = ZA * ZH
B = ZB * Y
LANES = 128
hard_weight = 4.0
logit_scale = 4.0 / math.sqrt(D)
bf16, f32 = jnp.bfloat16, jnp.float32
params = pltpu.CompilerParams(vmem_limit_bytes=40 * 2**20)
whole = pl.BlockSpec(memory_space=pltpu.VMEM)
scalars = pl.BlockSpec(memory_space=pltpu.SMEM)


def exchange(x, axes):
    return lax.all_to_all(x, axes, 0, 0, tiled=True)


def shift(x, axis, by):
    n = SIZES[axis]
    return lax.ppermute(x, axis, [(i, (i + by) % n) for i in range(n)])


def logits_kernel(at_ref, *refs):
    q_refs, (p_ref, out_ref, rows_ref) = refs[:X], refs[X:]
    n, k = q_refs[0].shape[2:]
    for j in range(X):
        for cc in range(C):
            g = lax.rem(at_ref[0] + X - j, X) * C + lax.rem(at_ref[1] + cc, C)
            for za in range(ZA):
                row = pl.multiple_of(g * (ZA * n) + za * n, n)
                for s in range(ZH):
                    rows_ref[pl.ds(row, n), s * k : (s + 1) * k] = q_refs[j][cc, za * ZH + s]
    out_ref[...] = lax.dot_general(
        rows_ref[...], p_ref[...], (((1,), (1,)), ((), ())), preferred_element_type=f32
    )


def softmax_kernel(part_ref, ids_ref, ds_ref):
    rows, n = part_ref.shape[1:]
    positive = ids_ref[:, 0:1]
    col = lax.broadcasted_iota(jnp.int32, (rows, n), 1)
    base = (
        (((col >> 3) & 1) << 10)
        + (((col >> 6) & 3) << 8)
        + (((col >> 1) & 3) << 3)
        + (((col >> 4) & 3) << 1)
        + (col & 1)
    )
    logits, top = [], None
    for g in range(G):
        a = part_ref[g * Y]
        for y in range(1, Y):
            a = a + part_ref[g * Y + y]
        a = a * logit_scale
        logits.append(a)
        m = jnp.max(a, axis=1, keepdims=True)
        top = m if top is None else jnp.maximum(top, m)
    total = jnp.zeros((rows, 1), f32)
    pos_logit = jnp.zeros((rows, 1), f32)
    scaled, hot = [], []
    for g in range(G):
        ids = base + g * 32
        onehot = ids == positive
        hard = ids == ids_ref[:, 1:2]
        for h in range(2, ids_ref.shape[1]):
            hard = jnp.logical_or(hard, ids == ids_ref[:, h : h + 1])
        hard = jnp.logical_and(hard, jnp.logical_not(onehot))
        e = jnp.where(hard, hard_weight, 1.0) * jnp.exp(logits[g] - top)
        total = total + jnp.sum(e, axis=1, keepdims=True)
        pos_logit = pos_logit + jnp.sum(jnp.where(onehot, logits[g], 0.0), axis=1, keepdims=True)
        scaled.append(e)
        hot.append(jnp.where(onehot, 1.0, 0.0))
    loss = top + jnp.log(total) - pos_logit
    hi = loss.astype(bf16).astype(f32)
    mid = (loss - hi).astype(bf16).astype(f32)
    lo = loss - hi - mid
    lane = lax.broadcasted_iota(jnp.int32, (rows, LANES), 1)
    side = jnp.where(lane == 0, hi, jnp.where(lane == 1, mid, jnp.where(lane == 2, lo, 0.0)))
    side = side.astype(bf16)
    for g in range(G):
        ds = (logit_scale * (scaled[g] / total - hot[g])).astype(bf16)
        for y in range(Y):
            ds_ref[g * Y + y, :, :n] = ds
            ds_ref[g * Y + y, :, n:] = side


def grads_kernel(at_ref, ds_ref, rows_ref, p_ref, *outs):
    qg_refs, (pg_ref, loss_ref) = outs[:X], outs[X:]
    n, k = qg_refs[0].shape[2:]
    np_ = p_ref.shape[0]
    for j in range(X):
        for cc in range(C):
            g = lax.rem(at_ref[0] + j, X) * C + lax.rem(at_ref[1] + cc, C)
            row = pl.multiple_of(g * (ZA * n), ZA * n)
            terms = jnp.dot(
                ds_ref[pl.ds(row, ZA * n), :np_], p_ref[...], preferred_element_type=f32
            ).astype(bf16)
            for za in range(ZA):
                for s in range(ZH):
                    qg_refs[j][cc, za * ZH + s] = terms[za * n : (za + 1) * n, s * k : (s + 1) * k]
            if j == 0 and cc == 0:
                loss_ref[...] = ds_ref[pl.ds(row, ZA * n), np_:]
    pg_ref[...] = lax.dot_general(
        ds_ref[:, :np_], rows_ref[...], (((0,), (0,)), ((), ())), preferred_element_type=f32
    ).astype(bf16)


def on_device(queries, passages, positive, hard_negs):
    nq, k = queries.shape
    own, d = passages.shape
    n = nq // A
    nrow = ZA * n // Y
    width = ZH * k
    za, zh, y = lax.axis_index("za"), lax.axis_index("zh"), lax.axis_index("y")
    at = jnp.stack([lax.axis_index("x"), lax.axis_index("c")]).astype(jnp.int32)

    ids = jnp.concatenate([positive[:, None], hard_negs], axis=1)
    half = lax.rem(y, 2) * nrow
    mine = lax.dynamic_slice_in_dim(ids, (za * ZH + zh) * n + half, nrow, 0)
    other = lax.dynamic_slice_in_dim(ids, ((1 - za) * ZH + zh) * n + half, nrow, 0)
    ids = jnp.where(y // 2 == za, mine, shift(other, "za", 1))

    prow = own * d // k
    send = jnp.concatenate(
        [
            queries.astype(bf16).reshape(A, n, k),
            jnp.broadcast_to(passages.astype(bf16).reshape(1, prow, k), (A, prow, k)),
        ],
        axis=1,
    )
    got = exchange(send, FAR)
    q = got[:, :n]
    theirs, p = lax.optimization_barrier((shift(q, "c", 1), got[:, n:]))
    both = jnp.stack([q, theirs])
    qs = [both] + [shift(both, "x", j) for j in range(1, X)]

    p = p.reshape(A, own, ZH, Y, k).transpose(3, 0, 1, 2, 4).reshape(Y, A * own, width)
    p = jnp.broadcast_to(p[None], (ZB,) + p.shape).reshape(B, A * own, width)
    p = exchange(p, NEAR).reshape(B * A * own, width)
    np_ = p.shape[0]

    parts, rows = pl.pallas_call(
        logits_kernel,
        in_specs=[scalars] + [whole] * (X + 1),
        out_specs=(whole, whole),
        out_shape=(
            jax.ShapeDtypeStruct((G * ZA * n, np_), f32),
            jax.ShapeDtypeStruct((G * ZA * n, width), bf16),
        ),
        compiler_params=params,
        name="logits",
    )(at, *qs, p)
    parts = exchange(parts.reshape(G * Y, nrow, np_), PLANE)

    ds = pl.pallas_call(
        softmax_kernel,
        out_shape=jax.ShapeDtypeStruct((G * Y, nrow, np_ + LANES), bf16),
        compiler_params=params,
        name="softmax",
    )(parts, ids)
    ds = exchange(ds, PLANE).reshape(G * ZA * n, np_ + LANES)

    *qg, pg, loss = pl.pallas_call(
        grads_kernel,
        in_specs=[scalars] + [whole] * 3,
        out_specs=tuple([whole] * (X + 2)),
        out_shape=tuple(
            [jax.ShapeDtypeStruct((C, A, n, k), bf16)] * X
            + [
                jax.ShapeDtypeStruct((np_, width), bf16),
                jax.ShapeDtypeStruct((ZA * n, LANES), bf16),
            ]
        ),
        compiler_params=params,
        name="grads",
    )(at, ds, rows, p)

    terms = [qg[0]] + [shift(qg[j], "x", j) for j in range(1, X)]
    pg = exchange(pg.reshape(B, A * own, width), NEAR)
    terms, pg = lax.optimization_barrier((terms, pg))
    pg = jnp.sum(pg.astype(f32).reshape(ZB, Y, A * own, width), axis=0).astype(bf16)
    pg = pg.reshape(Y, A, own, ZH, k).transpose(1, 2, 3, 0, 4).reshape(A, prow, k)
    pair = sum(t.astype(f32) for t in terms)
    theirs = shift(pair[1].astype(bf16), "c", 1)
    qg = (pair[0] + theirs.astype(f32)).astype(bf16)

    loss = loss.reshape(ZA, n, LANES)[:, :, :3].transpose(0, 2, 1).reshape(ZA, 1, 3 * n)
    loss = jnp.pad(loss, ((0, 0), (0, 7), (0, k - 3 * n)))
    loss = jnp.broadcast_to(loss[:, None], (ZA, ZH, 8, k)).reshape(A, 8, k)
    got = exchange(jnp.concatenate([qg, pg, loss], axis=1), FAR)
    qg = got[:, :n].reshape(nq, k).astype(f32)
    pg = jnp.sum(got[:, n : n + prow].astype(f32), axis=0).reshape(own, d)
    loss = got[:, n + prow, : 3 * n].astype(f32).reshape(A, 3, n)
    row_loss = (loss[:, 0] + loss[:, 1] + loss[:, 2]).reshape(nq)
    return row_loss, qg, pg


def solution(mesh):
    fine = Mesh(mesh.devices.reshape(*SIZES.values()), tuple(SIZES))
    dp, sub = ("za", "zb", "x", "c"), ("zh", "y")
    return jax.shard_map(
        on_device,
        mesh=fine,
        in_specs=(P(dp, sub), P(dp + sub, None), P(dp), P(dp, None)),
        out_specs=(P(dp), P(dp, sub), P(dp + sub, None)),
        check_vma=False,
    )
```

time: 317 us -> 222 us (0.70)
  the two profiles are of different devices: /device:TPU:2 before, /device:TPU:8 now
where the time goes in v2:
time: 222 us; the launch traced here: 221 us
  blocking collectives  129 us (58%)
  starting transfers between devices  54 us (24%)
  waiting for transfers between devices  26.3 us (12%)
  Pallas kernels  4.7 us (2%)
  local copies, waits for them, and re-layouts  3.72 us (2%)
  other arithmetic  3.02 us (1%)
    all_to_all x3, blocking collectives, exchange(): return lax.all_to_all(x, axes, 0, 0, tiled=True)  129 us
    ppermute x9, starting transfers between devices, shift(): return lax.ppermute(x, axis, [(i, (i + by) % n) for i in range(n)])  28.9 us
    ppermute x9, waiting for transfers between devices, shift(): return lax.ppermute(x, axis, [(i, (i + by) % n) for i in range(n)])  26.3 us
    all_to_all x3, starting transfers between devices, exchange(): return lax.all_to_all(x, axes, 0, 0, tiled=True)  25.1 us
  transfers between devices with their start and end apart: 12, of which 8 were waited for; matrix products, arithmetic and copies ran while one was open for 0% of the time, Pallas kernels for 0%

profile of v2, /device:TPU:8, one launch (start us, length us, event | category | flops | bytes accessed | tf_op | source)
XLA Modules:
  0.0 221.4 jit_solution(6162129395196594587)
XLA Ops:
  2.4 60.1 %all_to_all.30 = bf16[8,64,256]{2,1,0:T(8,128)(2,1)S(1)} all-to-all(bf16[8,64,256]{2,1,0:T(8,128)(2,1)S(1)} %pad_maximum_fusion.1), channel_id=1, replica_groups=mesh['za'=2,'zb'=4,'x'=4,'c'=2,'zh'=4,'y'=4] {'za','zh'}, dimensions={0} | all-to-all | bytes 524288 | tf_op jit(solution)/shard_map/all_to_all | solution.py:29
  62.6 1.9 collective-permute-start
  64.6 1.3 collective-permute-done
  66.9 12.4 %all-to-all-start.1 = ((bf16[16,16,1024]{2,1,0:T(8,128)(2,1)}), bf16[16,16,1024]{2,1,0:T(8,128)(2,1)S(1)}, u32[]{:S(2)}, u32[]{:S(2)}) async-start(bf16[16,16,1024]{2,1,0:T(8,128)(2,1)} %bitcast.6), calls=%async_computation.1 | async-start | bytes 1048576 | tf_op jit(solution)/shard_map/all_to_all | solution.py:29
  79.3 4.7 %collective-permute-start.3 = (bf16[2,8,32,256]{3,2,1,0:T(8,128)(2,1)S(1)}, bf16[2,8,32,256]{3,2,1,0:T(8,128)(2,1)S(1)}, u32[]{:S(2)}, u32[]{:S(2)}) collective-permute-start(bf16[2,8,32,256]{3,2,1,0:T(8,128)(2,1)S(1)} %pad_maximum_fusion.2.refs_0_), channel_id=1, source_target_pairs={{0,96},{32,0},{64,32},{96,64},{1,97},{33,1},{65,33},{97,65},{2,98}... | collective-permute-start | bytes 786440 | tf_op jit(solution)/shard_map/ppermute | solution.py:34
  84.0 2.7 %collective-permute-start.2 = (bf16[2,8,32,256]{3,2,1,0:T(8,128)(2,1)S(1)}, bf16[2,8,32,256]{3,2,1,0:T(8,128)(2,1)S(1)}, u32[]{:S(2)}, u32[]{:S(2)}) collective-permute-start(bf16[2,8,32,256]{3,2,1,0:T(8,128)(2,1)S(1)} %pad_maximum_fusion.2.refs_0_), channel_id=1, source_target_pairs={{0,64},{32,96},{64,0},{96,32},{1,65},{33,97},{65,1},{97,33},{2,66}... | collective-permute-start | bytes 786440 | tf_op jit(solution)/shard_map/ppermute | solution.py:34
  86.7 2.8 %collective-permute-start.1 = (bf16[2,8,32,256]{3,2,1,0:T(8,128)(2,1)S(1)}, bf16[2,8,32,256]{3,2,1,0:T(8,128)(2,1)S(1)}, u32[]{:S(2)}, u32[]{:S(2)}) collective-permute-start(bf16[2,8,32,256]{3,2,1,0:T(8,128)(2,1)S(1)} %pad_maximum_fusion.2.refs_0_), channel_id=1, source_target_pairs={{0,32},{32,64},{64,96},{96,0},{1,33},{33,65},{65,97},{97,1},{2,34}... | collective-permute-start | bytes 786440 | tf_op jit(solution)/shard_map/ppermute | solution.py:34
  89.6 5.3 %collective-permute-done.3.refs_3_ = bf16[2,8,32,256]{3,2,1,0:T(8,128)(2,1)S(1)} collective-permute-done((bf16[2,8,32,256]{3,2,1,0:T(8,128)(2,1)S(1)}, bf16[2,8,32,256]{3,2,1,0:T(8,128)(2,1)S(1)}, u32[]{:S(2)}, u32[]{:S(2)}) %collective-permute-start.3) | collective-permute-done | bytes 262176 | tf_op jit(solution)/shard_map/ppermute | solution.py:34
  94.9 1.7 collective-permute-done.2.refs_2_
  96.6 3.9 %collective-permute-done.1.refs_1_ = bf16[2,8,32,256]{3,2,1,0:T(8,128)(2,1)S(1)} collective-permute-done((bf16[2,8,32,256]{3,2,1,0:T(8,128)(2,1)S(1)}, bf16[2,8,32,256]{3,2,1,0:T(8,128)(2,1)S(1)}, u32[]{:S(2)}, u32[]{:S(2)}) %collective-permute-start.1) | collective-permute-done | bytes 262176 | tf_op jit(solution)/shard_map/ppermute | solution.py:34
  100.5 1.8 logits.1
  102.3 5.2 %all-to-all-start.2 = ((f32[32,16,256]{2,1,0:T(8,128)}), f32[32,16,256]{2,1,0:T(8,128)S(1)}, u32[]{:S(2)}, u32[]{:S(2)}) async-start(f32[32,16,256]{2,1,0:T(8,128)} %bitcast.8), calls=%async_computation.2 | async-start | bytes 1048576 | tf_op jit(solution)/shard_map/all_to_all | solution.py:29
  108.4 5.0 %collective-permute-start.4 = (s32[16,5]{1,0:T(8,128)S(1)}, s32[16,5]{1,0:T(8,128)S(1)}, u32[]{:S(2)}, u32[]{:S(2)}) collective-permute-start(s32[16,5]{1,0:T(8,128)S(1)} %copy.21), channel_id=1, source_target_pairs={{0,512},{512,0},{1,513},{513,1},{2,514},{514,2},{3,515},{515,3},{4... | collective-permute-start | bytes 968 | tf_op jit(solution)/shard_map/ppermute | solution.py:34
  113.5 4.3 %collective-permute-done.4 = s32[16,5]{1,0:T(8,128)S(1)} collective-permute-done((s32[16,5]{1,0:T(8,128)S(1)}, s32[16,5]{1,0:T(8,128)S(1)}, u32[]{:S(2)}, u32[]{:S(2)}) %collective-permute-start.4) | collective-permute-done | bytes 352 | tf_op jit(solution)/shard_map/ppermute | solution.py:34
  118.2 15.5 %all_to_all.31 = bf16[32,16,384]{2,1,0:T(8,128)(2,1)S(1)} all-to-all(bf16[32,16,384]{2,1,0:T(8,128)(2,1)S(1)} %softmax.1), channel_id=1, replica_groups=mesh['za'=2,'zb'=4,'x'=4,'c'=2,'zh'=4,'y'=4] {'x','c','y'}, dimensions={0} | all-to-all | bytes 786432 | tf_op jit(solution)/shard_map/all_to_all | solution.py:29
  133.7 2.5 %grads.1 = (bf16[2,8,32,256]{3,2,1,0:T(8,128)(2,1)S(1)}, bf16[2,8,32,256]{3,2,1,0:T(8,128)(2,1)S(1)}, bf16[2,8,32,256]{3,2,1,0:T(8,128)(2,1)S(1)}, bf16[2,8,32,2...) custom-call(s32[2]{0:T(128)S(1)} %pad_add_fusion.at_ref, ...), custom_call_target="tpu_custom_call" | custom-call | tf_op jit(solution)/shard_map/grads/pallas_call | solution.py:177
  136.2 7.5 %all-to-all-start.4 = ((bf16[16,16,1024]{2,1,0:T(8,128)(2,1)}), bf16[16,16,1024]{2,1,0:T(8,128)(2,1)S(1)}, u32[]{:S(2)}, u32[]{:S(2)}) async-start(bf16[16,16,1024]{2,1,0:T(8,128)(2,1)} %bitcast.11), calls=%async_computation.4 | async-start | bytes 1048576 | tf_op jit(solution)/shard_map/all_to_all | solution.py:29
  143.8 2.7 %collective-permute-start.5 = (bf16[2,8,32,256]{3,2,1,0:T(8,128)(2,1)S(1)}, bf16[2,8,32,256]{3,2,1,0:T(8,128)(2,1)S(1)}, u32[]{:S(2)}, u32[]{:S(2)}) collective-permute-start(bf16[2,8,32,256]{3,2,1,0:T(8,128)(2,1)S(1)} %get-tuple-element.23), channel_id=1, source_target_pairs={{0,32},{32,64},{64,96},{96,0},{1,33},{33,65},{65,97},{97,1},{2,34}... | collective-permute-start | bytes 786440 | tf_op jit(solution)/shard_map/ppermute | solution.py:34
  146.5 3.9 %collective-permute-start.6 = (bf16[2,8,32,256]{3,2,1,0:T(8,128)(2,1)S(1)}, bf16[2,8,32,256]{3,2,1,0:T(8,128)(2,1)S(1)}, u32[]{:S(2)}, u32[]{:S(2)}) collective-permute-start(bf16[2,8,32,256]{3,2,1,0:T(8,128)(2,1)S(1)} %get-tuple-element.24), channel_id=1, source_target_pairs={{0,64},{32,96},{64,0},{96,32},{1,65},{33,97},{65,1},{97,33},{2,66}... | collective-permute-start | bytes 786440 | tf_op jit(solution)/shard_map/ppermute | solution.py:34
  150.4 3.3 %collective-permute-start.7 = (bf16[2,8,32,256]{3,2,1,0:T(8,128)(2,1)S(1)}, bf16[2,8,32,256]{3,2,1,0:T(8,128)(2,1)S(1)}, u32[]{:S(2)}, u32[]{:S(2)}) collective-permute-start(bf16[2,8,32,256]{3,2,1,0:T(8,128)(2,1)S(1)} %get-tuple-element.25), channel_id=1, source_target_pairs={{0,96},{32,0},{64,32},{96,64},{1,97},{33,1},{65,33},{97,65},{2,98}... | collective-permute-start | bytes 786440 | tf_op jit(solution)/shard_map/ppermute | solution.py:34
  153.7 6.4 %collective-permute-done.5 = bf16[2,8,32,256]{3,2,1,0:T(8,128)(2,1)S(1)} collective-permute-done((bf16[2,8,32,256]{3,2,1,0:T(8,128)(2,1)S(1)}, bf16[2,8,32,256]{3,2,1,0:T(8,128)(2,1)S(1)}, u32[]{:S(2)}, u32[]{:S(2)}) %collective-permute-start.5) | collective-permute-done | bytes 262176 | tf_op jit(solution)/shard_map/ppermute | solution.py:34
  160.1 2.5 %collective-permute-done.7 = bf16[2,8,32,256]{3,2,1,0:T(8,128)(2,1)S(1)} collective-permute-done((bf16[2,8,32,256]{3,2,1,0:T(8,128)(2,1)S(1)}, bf16[2,8,32,256]{3,2,1,0:T(8,128)(2,1)S(1)}, u32[]{:S(2)}, u32[]{:S(2)}) %collective-permute-start.7) | collective-permute-done | bytes 262176 | tf_op jit(solution)/shard_map/ppermute | solution.py:34
  162.8 1.9 collective-permute-start.8
  166.1 53.1 %all_to_all.32 = bf16[8,72,256]{2,1,0:T(8,128)(2,1)S(1)} all-to-all(bf16[8,72,256]{2,1,0:T(8,128)(2,1)S(1)} %pad_maximum_fusion), channel_id=1, replica_groups=mesh['za'=2,'zb'=4,'x'=4,'c'=2,'zh'=4,'y'=4] {'za','zh'}, dimensions={0} | all-to-all | bytes 589824 | tf_op jit(solution)/shard_map/all_to_all | solution.py:29
  (46 shorter events, 7.9 us)
Async XLA Ops:
  62.6 3.2 %collective-permute-start = (bf16[8,32,256]{2,1,0:T(8,128)(2,1)S(1)}, bf16[8,32,256]{2,1,0:T(8,128)(2,1)S(1)}, u32[]{:S(2)}, u32[]{:S(2)}) collective-permute-start(bf16[8,32,256]{2,1,0:T(8,128)(2,1)S(1)} %get-tuple-element.35), channel_id=1, source_target_pairs={{0,16},{16,0},{1,17},{17,1},{2,18},{18,2},{3,19},{19,3},{4,20},{20... | collective-permute-start | bytes 393224 | tf_op jit(solution)/shard_map/ppermute | solution.py:34
  66.9 33.6 %all-to-all-start.1 = ((bf16[16,16,1024]{2,1,0:T(8,128)(2,1)}), bf16[16,16,1024]{2,1,0:T(8,128)(2,1)S(1)}, u32[]{:S(2)}, u32[]{:S(2)}) async-start(bf16[16,16,1024]{2,1,0:T(8,128)(2,1)} %bitcast.6), calls=%async_computation.1 | async-start | bytes 1048576 | tf_op jit(solution)/shard_map/all_to_all | solution.py:29
  79.3 15.6 %collective-permute-start.3 = (bf16[2,8,32,256]{3,2,1,0:T(8,128)(2,1)S(1)}, bf16[2,8,32,256]{3,2,1,0:T(8,128)(2,1)S(1)}, u32[]{:S(2)}, u32[]{:S(2)}) collective-permute-start(bf16[2,8,32,256]{3,2,1,0:T(8,128)(2,1)S(1)} %pad_maximum_fusion.2.refs_0_), channel_id=1, source_target_pairs={{0,96},{32,0},{64,32},{96,64},{1,97},{33,1},{65,33},{97,65},{2,98}... | collective-permute-start | bytes 786440 | tf_op jit(solution)/shard_map/ppermute | solution.py:34
  84.0 12.7 %collective-permute-start.2 = (bf16[2,8,32,256]{3,2,1,0:T(8,128)(2,1)S(1)}, bf16[2,8,32,256]{3,2,1,0:T(8,128)(2,1)S(1)}, u32[]{:S(2)}, u32[]{:S(2)}) collective-permute-start(bf16[2,8,32,256]{3,2,1,0:T(8,128)(2,1)S(1)} %pad_maximum_fusion.2.refs_0_), channel_id=1, source_target_pairs={{0,64},{32,96},{64,0},{96,32},{1,65},{33,97},{65,1},{97,33},{2,66}... | collective-permute-start | bytes 786440 | tf_op jit(solution)/shard_map/ppermute | solution.py:34
  86.7 13.8 %collective-permute-start.1 = (bf16[2,8,32,256]{3,2,1,0:T(8,128)(2,1)S(1)}, bf16[2,8,32,256]{3,2,1,0:T(8,128)(2,1)S(1)}, u32[]{:S(2)}, u32[]{:S(2)}) collective-permute-start(bf16[2,8,32,256]{3,2,1,0:T(8,128)(2,1)S(1)} %pad_maximum_fusion.2.refs_0_), channel_id=1, source_target_pairs={{0,32},{32,64},{64,96},{96,0},{1,33},{33,65},{65,97},{97,1},{2,34}... | collective-permute-start | bytes 786440 | tf_op jit(solution)/shard_map/ppermute | solution.py:34
  102.3 15.5 %all-to-all-start.2 = ((f32[32,16,256]{2,1,0:T(8,128)}), f32[32,16,256]{2,1,0:T(8,128)S(1)}, u32[]{:S(2)}, u32[]{:S(2)}) async-start(f32[32,16,256]{2,1,0:T(8,128)} %bitcast.8), calls=%async_computation.2 | async-start | bytes 1048576 | tf_op jit(solution)/shard_map/all_to_all | solution.py:29
  107.6 0.7 copy-start
  107.6 0.7 copy-start.1
  108.4 9.5 %collective-permute-start.4 = (s32[16,5]{1,0:T(8,128)S(1)}, s32[16,5]{1,0:T(8,128)S(1)}, u32[]{:S(2)}, u32[]{:S(2)}) collective-permute-start(s32[16,5]{1,0:T(8,128)S(1)} %copy.21), channel_id=1, source_target_pairs={{0,512},{512,0},{1,513},{513,1},{2,514},{514,2},{3,515},{515,3},{4... | collective-permute-start | bytes 968 | tf_op jit(solution)/shard_map/ppermute | solution.py:34
  136.2 26.4 %all-to-all-start.4 = ((bf16[16,16,1024]{2,1,0:T(8,128)(2,1)}), bf16[16,16,1024]{2,1,0:T(8,128)(2,1)S(1)}, u32[]{:S(2)}, u32[]{:S(2)}) async-start(bf16[16,16,1024]{2,1,0:T(8,128)(2,1)} %bitcast.11), calls=%async_computation.4 | async-start | bytes 1048576 | tf_op jit(solution)/shard_map/all_to_all | solution.py:29
  143.8 16.3 %collective-permute-start.5 = (bf16[2,8,32,256]{3,2,1,0:T(8,128)(2,1)S(1)}, bf16[2,8,32,256]{3,2,1,0:T(8,128)(2,1)S(1)}, u32[]{:S(2)}, u32[]{:S(2)}) collective-permute-start(bf16[2,8,32,256]{3,2,1,0:T(8,128)(2,1)S(1)} %get-tuple-element.23), channel_id=1, source_target_pairs={{0,32},{32,64},{64,96},{96,0},{1,33},{33,65},{65,97},{97,1},{2,34}... | collective-permute-start | bytes 786440 | tf_op jit(solution)/shard_map/ppermute | solution.py:34
  146.5 13.6 %collective-permute-start.6 = (bf16[2,8,32,256]{3,2,1,0:T(8,128)(2,1)S(1)}, bf16[2,8,32,256]{3,2,1,0:T(8,128)(2,1)S(1)}, u32[]{:S(2)}, u32[]{:S(2)}) collective-permute-start(bf16[2,8,32,256]{3,2,1,0:T(8,128)(2,1)S(1)} %get-tuple-element.24), channel_id=1, source_target_pairs={{0,64},{32,96},{64,0},{96,32},{1,65},{33,97},{65,1},{97,33},{2,66}... | collective-permute-start | bytes 786440 | tf_op jit(solution)/shard_map/ppermute | solution.py:34
  150.4 12.2 %collective-permute-start.7 = (bf16[2,8,32,256]{3,2,1,0:T(8,128)(2,1)S(1)}, bf16[2,8,32,256]{3,2,1,0:T(8,128)(2,1)S(1)}, u32[]{:S(2)}, u32[]{:S(2)}) collective-permute-start(bf16[2,8,32,256]{3,2,1,0:T(8,128)(2,1)S(1)} %get-tuple-element.25), channel_id=1, source_target_pairs={{0,96},{32,0},{64,32},{96,64},{1,97},{33,1},{65,33},{97,65},{2,98}... | collective-permute-start | bytes 786440 | tf_op jit(solution)/shard_map/ppermute | solution.py:34
  162.8 3.2 %collective-permute-start.8 = (bf16[8,32,256]{2,1,0:T(8,128)(2,1)S(1)}, bf16[8,32,256]{2,1,0:T(8,128)(2,1)S(1)}, u32[]{:S(2)}, u32[]{:S(2)}) collective-permute-start(bf16[8,32,256]{2,1,0:T(8,128)(2,1)S(1)} %fusion.2), channel_id=1, source_target_pairs={{0,16},{16,0},{1,17},{17,1},{2,18},{18,2},{3,19},{19,3},{4,20},{20... | collective-permute-start | bytes 393224 | tf_op jit(solution)/shard_map/ppermute | solution.py:34

commit v3 on v2

--- a/solution.py
+++ b/solution.py
@@ -35,21 +35,22 @@
 
 
 def logits_kernel(at_ref, *refs):
-    q_refs, (p_ref, out_ref, rows_ref) = refs[:X], refs[X:]
-    n, k = q_refs[0].shape[2:]
+    mine, theirs, (first_ref, p_ref, out_ref, rows_ref) = refs[:X], refs[X], refs[X + 1 :]
+    n, k = first_ref.shape[1:]
     for j in range(X):
         for cc in range(C):
             g = lax.rem(at_ref[0] + X - j, X) * C + lax.rem(at_ref[1] + cc, C)
+            block = mine[j] if cc == 0 else first_ref if j == 0 else theirs.at[j - 1]
             for za in range(ZA):
                 row = pl.multiple_of(g * (ZA * n) + za * n, n)
                 for s in range(ZH):
-                    rows_ref[pl.ds(row, n), s * k : (s + 1) * k] = q_refs[j][cc, za * ZH + s]
+                    rows_ref[pl.ds(row, n), s * k : (s + 1) * k] = block[za * ZH + s]
     out_ref[...] = lax.dot_general(
         rows_ref[...], p_ref[...], (((1,), (1,)), ((), ())), preferred_element_type=f32
     )
 
 
-def softmax_kernel(part_ref, ids_ref, ds_ref):
+def softmax_kernel(part_ref, ids_ref, ds_ref, side_ref):
     rows, n = part_ref.shape[1:]
     positive = ids_ref[:, 0:1]
     col = lax.broadcasted_iota(jnp.int32, (rows, n), 1)
@@ -90,33 +91,32 @@
     lo = loss - hi - mid
     lane = lax.broadcasted_iota(jnp.int32, (rows, LANES), 1)
     side = jnp.where(lane == 0, hi, jnp.where(lane == 1, mid, jnp.where(lane == 2, lo, 0.0)))
-    side = side.astype(bf16)
+    side_ref[...] = side.astype(bf16)
     for g in range(G):
         ds = (logit_scale * (scaled[g] / total - hot[g])).astype(bf16)
         for y in range(Y):
-            ds_ref[g * Y + y, :, :n] = ds
-            ds_ref[g * Y + y, :, n:] = side
-
-
-def grads_kernel(at_ref, ds_ref, rows_ref, p_ref, *outs):
-    qg_refs, (pg_ref, loss_ref) = outs[:X], outs[X:]
-    n, k = qg_refs[0].shape[2:]
-    np_ = p_ref.shape[0]
-    for j in range(X):
-        for cc in range(C):
+            ds_ref[g * Y + y] = ds
+
+
+def grads_kernel(at_ref, ds_ref, side_ref, rows_ref, p_ref, qg_ref, pg_ref):
+    n, k = qg_ref.shape[3:]
+    width = rows_ref.shape[1]
+    for cc in range(C):
+        for j in range(X):
             g = lax.rem(at_ref[0] + j, X) * C + lax.rem(at_ref[1] + cc, C)
             row = pl.multiple_of(g * (ZA * n), ZA * n)
             terms = jnp.dot(
-                ds_ref[pl.ds(row, ZA * n), :np_], p_ref[...], preferred_element_type=f32
+                ds_ref[pl.ds(row, ZA * n), :], p_ref[...], preferred_element_type=f32
             ).astype(bf16)
             for za in range(ZA):
                 for s in range(ZH):
-                    qg_refs[j][cc, za * ZH + s] = terms[za * n : (za + 1) * n, s * k : (s + 1) * k]
-            if j == 0 and cc == 0:
-                loss_ref[...] = ds_ref[pl.ds(row, ZA * n), np_:]
-    pg_ref[...] = lax.dot_general(
-        ds_ref[:, :np_], rows_ref[...], (((0,), (0,)), ((), ())), preferred_element_type=f32
+                    qg_ref[cc, j, za * ZH + s] = terms[za * n : (za + 1) * n, s * k : (s + 1) * k]
+    pg_ref[:, :width] = lax.dot_general(
+        ds_ref[...], rows_ref[...], (((0,), (0,)), ((), ())), preferred_element_type=f32
     ).astype(bf16)
+    nrow = side_ref.shape[0]
+    for b in range(pg_ref.shape[0] // nrow):
+        pg_ref[b * nrow : (b + 1) * nrow, width:] = side_ref[...]
 
 
 def on_device(queries, passages, positive, hard_negs):
@@ -144,18 +144,18 @@
     )
     got = exchange(send, FAR)
     q = got[:, :n]
-    theirs, p = lax.optimization_barrier((shift(q, "c", 1), got[:, n:]))
-    both = jnp.stack([q, theirs])
-    qs = [both] + [shift(both, "x", j) for j in range(1, X)]
-
-    p = p.reshape(A, own, ZH, Y, k).transpose(3, 0, 1, 2, 4).reshape(Y, A * own, width)
+    qs = [q] + [shift(q, "x", j) for j in range(1, X)]
+    first = shift(q, "c", 1)
+    theirs = shift(jnp.stack(qs[1:]), "c", 1)
+
+    p = got[:, n:].reshape(A, own, ZH, Y, k).transpose(3, 0, 1, 2, 4).reshape(Y, A * own, width)
     p = jnp.broadcast_to(p[None], (ZB,) + p.shape).reshape(B, A * own, width)
     p = exchange(p, NEAR).reshape(B * A * own, width)
     np_ = p.shape[0]
 
     parts, rows = pl.pallas_call(
         logits_kernel,
-        in_specs=[scalars] + [whole] * (X + 1),
+        in_specs=[scalars] + [whole] * (X + 3),
         out_specs=(whole, whole),
         out_shape=(
             jax.ShapeDtypeStruct((G * ZA * n, np_), f32),
@@ -163,42 +163,43 @@
         ),
         compiler_params=params,
         name="logits",
-    )(at, *qs, p)
+    )(at, *qs, theirs, first, p)
     parts = exchange(parts.reshape(G * Y, nrow, np_), PLANE)
 
-    ds = pl.pallas_call(
+    ds, side = pl.pallas_call(
         softmax_kernel,
-        out_shape=jax.ShapeDtypeStruct((G * Y, nrow, np_ + LANES), bf16),
+        out_shape=(
+            jax.ShapeDtypeStruct((G * Y, nrow, np_), bf16),
+            jax.ShapeDtypeStruct((nrow, LANES), bf16),
+        ),
         compiler_params=params,
         name="softmax",
     )(parts, ids)
-    ds = exchange(ds, PLANE).reshape(G * ZA * n, np_ + LANES)
-
-    *qg, pg, loss = pl.pallas_call(
+    ds = exchange(ds, PLANE).reshape(G * ZA * n, np_)
+
+    qg, pg = pl.pallas_call(
         grads_kernel,
-        in_specs=[scalars] + [whole] * 3,
-        out_specs=tuple([whole] * (X + 2)),
-        out_shape=tuple(
-            [jax.ShapeDtypeStruct((C, A, n, k), bf16)] * X
-            + [
-                jax.ShapeDtypeStruct((np_, width), bf16),
-                jax.ShapeDtypeStruct((ZA * n, LANES), bf16),
-            ]
+        in_specs=[scalars] + [whole] * 4,
+        out_specs=(whole, whole),
+        out_shape=(
+            jax.ShapeDtypeStruct((C, X, A, n, k), bf16),
+            jax.ShapeDtypeStruct((np_, width + LANES), bf16),
         ),
         compiler_params=params,
         name="grads",
-    )(at, ds, rows, p)
-
-    terms = [qg[0]] + [shift(qg[j], "x", j) for j in range(1, X)]
-    pg = exchange(pg.reshape(B, A * own, width), NEAR)
+    )(at, ds, side, rows, p)
+
+    pg = exchange(pg.reshape(B, A * own, width + LANES), NEAR)
+    pair = (qg[0].astype(f32) + shift(qg[1], "c", 1).astype(f32)).astype(bf16)
+    terms = [pair[0]] + [shift(pair[j], "x", j) for j in range(1, X)]
     terms, pg = lax.optimization_barrier((terms, pg))
-    pg = jnp.sum(pg.astype(f32).reshape(ZB, Y, A * own, width), axis=0).astype(bf16)
+    qg = sum(t.astype(f32) for t in terms).astype(bf16)
+    side = lax.dynamic_slice_in_dim(pg, lax.axis_index("zb") * Y, Y, 0)[:, :, width : width + 3]
+    pg = pg[:, :, :width].astype(f32).reshape(ZB, Y, A * own, width)
+    pg = jnp.sum(pg, axis=0).astype(bf16)
     pg = pg.reshape(Y, A, own, ZH, k).transpose(1, 2, 3, 0, 4).reshape(A, prow, k)
-    pair = sum(t.astype(f32) for t in terms)
-    theirs = shift(pair[1].astype(bf16), "c", 1)
-    qg = (pair[0] + theirs.astype(f32)).astype(bf16)
-
-    loss = loss.reshape(ZA, n, LANES)[:, :, :3].transpose(0, 2, 1).reshape(ZA, 1, 3 * n)
+
+    loss = side.reshape(ZA, n, 3).transpose(0, 2, 1).reshape(ZA, 1, 3 * n)
     loss = jnp.pad(loss, ((0, 0), (0, 7), (0, k - 3 * n)))
     loss = jnp.broadcast_to(loss[:, None], (ZA, ZH, 8, k)).reshape(A, 8, k)
     got = exchange(jnp.concatenate([qg, pg, loss], axis=1), FAR)

time: 222 us -> 214 us (0.964)
  the two profiles are of different devices: /device:TPU:8 before, /device:TPU:14 now
where the time goes in v3:
time: 214 us; the launch traced here: 213 us
  blocking collectives  125 us (58%)
  starting transfers between devices  56.2 us (26%)
  waiting for transfers between devices  19.3 us (9%)
  Pallas kernels  4.71 us (2%)
  local copies, waits for them, and re-layouts  3.85 us (2%)
  other arithmetic  3.11 us (1%)
    all_to_all x3, blocking collectives, exchange(): return lax.all_to_all(x, axes, 0, 0, tiled=True)  125 us
    ppermute x10, starting transfers between devices, shift(): return lax.ppermute(x, axis, [(i, (i + by) % n) for i in range(n)])  29.1 us
    all_to_all x3, starting transfers between devices, exchange(): return lax.all_to_all(x, axes, 0, 0, tiled=True)  27 us
    ppermute x10, waiting for transfers between devices, shift(): return lax.ppermute(x, axis, [(i, (i + by) % n) for i in range(n)])  19.3 us
  transfers between devices with their start and end apart: 13, of which 7 were waited for; matrix products, arithmetic and copies ran while one was open for 0% of the time, Pallas kernels for 0%

profile of v3, /device:TPU:14, one launch (start us, length us, event | category | flops | bytes accessed | tf_op | source)
XLA Modules:
  0.0 213.3 jit_solution(3494653363162030778)
XLA Ops:
  2.4 60.1 %all_to_all.30 = bf16[8,64,256]{2,1,0:T(8,128)(2,1)S(1)} all-to-all(bf16[8,64,256]{2,1,0:T(8,128)(2,1)S(1)} %pad_maximum_fusion.2), channel_id=1, replica_groups=mesh['za'=2,'zb'=4,'x'=4,'c'=2,'zh'=4,'y'=4] {'za','zh'}, dimensions={0} | all-to-all | bytes 524288 | tf_op jit(solution)/shard_map/all_to_all | solution.py:29
  63.7 12.4 %all-to-all-start.1 = ((bf16[16,16,1024]{2,1,0:T(8,128)(2,1)}), bf16[16,16,1024]{2,1,0:T(8,128)(2,1)S(1)}, u32[]{:S(2)}, u32[]{:S(2)}) async-start(bf16[16,16,1024]{2,1,0:T(8,128)(2,1)} %bitcast.7), calls=%async_computation.1 | async-start | bytes 1048576 | tf_op jit(solution)/shard_map/all_to_all | solution.py:29
  76.0 2.4 %collective-permute-start = (bf16[8,32,256]{2,1,0:T(8,128)(2,1)S(1)}, bf16[8,32,256]{2,1,0:T(8,128)(2,1)S(1)}, u32[]{:S(2)}, u32[]{:S(2)}) collective-permute-start(bf16[8,32,256]{2,1,0:T(8,128)(2,1)S(1)} %get-tuple-element.30.refs_0_), channel_id=1, source_target_pairs={{0,32},{32,64},{64,96},{96,0},{1,33},{33,65},{65,97},{97,1},{2,34}... | collective-permute-start | bytes 393224 | tf_op jit(solution)/shard_map/ppermute | solution.py:34
  78.4 4.3 %collective-permute-start.1 = (bf16[8,32,256]{2,1,0:T(8,128)(2,1)S(1)}, bf16[8,32,256]{2,1,0:T(8,128)(2,1)S(1)}, u32[]{:S(2)}, u32[]{:S(2)}) collective-permute-start(bf16[8,32,256]{2,1,0:T(8,128)(2,1)S(1)} %get-tuple-element.30.refs_0_), channel_id=1, source_target_pairs={{0,64},{32,96},{64,0},{96,32},{1,65},{33,97},{65,1},{97,33},{2,66}... | collective-permute-start | bytes 393224 | tf_op jit(solution)/shard_map/ppermute | solution.py:34
  82.7 1.9 collective-permute-start.2
  84.7 2.7 %collective-permute-done.1.refs_2_ = bf16[8,32,256]{2,1,0:T(8,128)(2,1)S(1)} collective-permute-done((bf16[8,32,256]{2,1,0:T(8,128)(2,1)S(1)}, bf16[8,32,256]{2,1,0:T(8,128)(2,1)S(1)}, u32[]{:S(2)}, u32[]{:S(2)}) %collective-permute-start.1) | collective-permute-done | bytes 131104 | tf_op jit(solution)/shard_map/ppermute | solution.py:34
  87.4 3.4 %collective-permute-done.2.refs_3_ = bf16[8,32,256]{2,1,0:T(8,128)(2,1)S(1)} collective-permute-done((bf16[8,32,256]{2,1,0:T(8,128)(2,1)S(1)}, bf16[8,32,256]{2,1,0:T(8,128)(2,1)S(1)}, u32[]{:S(2)}, u32[]{:S(2)}) %collective-permute-start.2) | collective-permute-done | bytes 131104 | tf_op jit(solution)/shard_map/ppermute | solution.py:34
  90.9 1.9 collective-permute-start.3
  92.8 2.4 %collective-permute-start.4 = (bf16[8,32,256]{2,1,0:T(8,128)(2,1)S(1)}, bf16[8,32,256]{2,1,0:T(8,128)(2,1)S(1)}, u32[]{:S(2)}, u32[]{:S(2)}) collective-permute-start(bf16[8,32,256]{2,1,0:T(8,128)(2,1)S(1)} %get-tuple-element.30.refs_0_), channel_id=1, source_target_pairs={{0,16},{16,0},{1,17},{17,1},{2,18},{18,2},{3,19},{19,3},{4,20},{20... | collective-permute-start | bytes 393224 | tf_op jit(solution)/shard_map/ppermute | solution.py:34
  96.2 1.8 logits.1
  98.0 7.1 %all-to-all-start.2 = ((f32[32,16,256]{2,1,0:T(8,128)}), f32[32,16,256]{2,1,0:T(8,128)S(1)}, u32[]{:S(2)}, u32[]{:S(2)}) async-start(f32[32,16,256]{2,1,0:T(8,128)} %bitcast.9), calls=%async_computation.2 | async-start | bytes 1048576 | tf_op jit(solution)/shard_map/all_to_all | solution.py:29
  106.0 5.0 %collective-permute-start.5 = (s32[16,5]{1,0:T(8,128)S(1)}, s32[16,5]{1,0:T(8,128)S(1)}, u32[]{:S(2)}, u32[]{:S(2)}) collective-permute-start(s32[16,5]{1,0:T(8,128)S(1)} %copy.32), channel_id=1, source_target_pairs={{0,512},{512,0},{1,513},{513,1},{2,514},{514,2},{3,515},{515,3},{4... | collective-permute-start | bytes 968 | tf_op jit(solution)/shard_map/ppermute | solution.py:34
  111.1 4.4 %collective-permute-done.5 = s32[16,5]{1,0:T(8,128)S(1)} collective-permute-done((s32[16,5]{1,0:T(8,128)S(1)}, s32[16,5]{1,0:T(8,128)S(1)}, u32[]{:S(2)}, u32[]{:S(2)}) %collective-permute-start.5) | collective-permute-done | bytes 352 | tf_op jit(solution)/shard_map/ppermute | solution.py:34
  115.8 12.8 %all_to_all.31 = bf16[32,16,256]{2,1,0:T(8,128)(2,1)S(1)} all-to-all(bf16[32,16,256]{2,1,0:T(8,128)(2,1)S(1)} %get-tuple-element.15), channel_id=1, replica_groups=mesh['za'=2,'zb'=4,'x'=4,'c'=2,'zh'=4,'y'=4] {'x','c','y'}, dimensions={0} | all-to-all | bytes 524288 | tf_op jit(solution)/shard_map/all_to_all | solution.py:29
  128.6 2.6 %grads.1 = (bf16[2,4,8,32,256]{4,3,2,1,0:T(8,128)(2,1)S(1)}, bf16[256,1152]{1,0:T(8,128)(2,1)}) custom-call(s32[2]{0:T(128)S(1)} %pad_add_fusion.at_ref, bf16[512,256]{1,0:T(8,128)(2,1)S(1)} %bitcast.38, bf16[16,128]{1,0:T(8,128)(2,1)S(1)} %get-tuple-element.16.side_ref, bf16[512,1024]{1,0:T(8,128)(2,1)S(1)} %get-tuple-element.17.rows_ref, ...), custom_call_target="tpu_custom_call" | custom-call | tf_op jit(solution)/shard_map/grads/pallas_call | solution.py:180
  131.2 7.5 %all-to-all-start.4 = ((bf16[16,16,1152]{2,1,0:T(8,128)(2,1)}), bf16[16,16,1152]{2,1,0:T(8,128)(2,1)S(1)}, u32[]{:S(2)}, u32[]{:S(2)}) async-start(bf16[16,16,1152]{2,1,0:T(8,128)(2,1)} %bitcast.18), calls=%async_computation.4 | async-start | bytes 1179648 | tf_op jit(solution)/shard_map/all_to_all | solution.py:29
  138.8 1.9 collective-permute-start.6
  140.7 1.9 collective-permute-done.6
  142.8 3.9 %collective-permute-start.7 = (bf16[8,32,256]{2,1,0:T(8,128)(2,1)S(1)}, bf16[8,32,256]{2,1,0:T(8,128)(2,1)S(1)}, u32[]{:S(2)}, u32[]{:S(2)}) collective-permute-start(bf16[8,32,256]{2,1,0:T(8,128)(2,1)S(1)} %get-tuple-element.27), channel_id=1, source_target_pairs={{0,32},{32,64},{64,96},{96,0},{1,33},{33,65},{65,97},{97,1},{2,34}... | collective-permute-start | bytes 393224 | tf_op jit(solution)/shard_map/ppermute | solution.py:34
  146.7 2.7 %collective-permute-start.8 = (bf16[8,32,256]{2,1,0:T(8,128)(2,1)S(1)}, bf16[8,32,256]{2,1,0:T(8,128)(2,1)S(1)}, u32[]{:S(2)}, u32[]{:S(2)}) collective-permute-start(bf16[8,32,256]{2,1,0:T(8,128)(2,1)S(1)} %get-tuple-element.26), channel_id=1, source_target_pairs={{0,64},{32,96},{64,0},{96,32},{1,65},{33,97},{65,1},{97,33},{2,66}... | collective-permute-start | bytes 393224 | tf_op jit(solution)/shard_map/ppermute | solution.py:34
  149.4 2.7 %collective-permute-start.9 = (bf16[8,32,256]{2,1,0:T(8,128)(2,1)S(1)}, bf16[8,32,256]{2,1,0:T(8,128)(2,1)S(1)}, u32[]{:S(2)}, u32[]{:S(2)}) collective-permute-start(bf16[8,32,256]{2,1,0:T(8,128)(2,1)S(1)} %get-tuple-element.25), channel_id=1, source_target_pairs={{0,96},{32,0},{64,32},{96,64},{1,97},{33,1},{65,33},{97,65},{2,98}... | collective-permute-start | bytes 393224 | tf_op jit(solution)/shard_map/ppermute | solution.py:34
  152.1 3.8 %collective-permute-done.8 = bf16[8,32,256]{2,1,0:T(8,128)(2,1)S(1)} collective-permute-done((bf16[8,32,256]{2,1,0:T(8,128)(2,1)S(1)}, bf16[8,32,256]{2,1,0:T(8,128)(2,1)S(1)}, u32[]{:S(2)}, u32[]{:S(2)}) %collective-permute-start.8) | collective-permute-done | bytes 131104 | tf_op jit(solution)/shard_map/ppermute | solution.py:34
  155.9 2.3 %collective-permute-done.9 = bf16[8,32,256]{2,1,0:T(8,128)(2,1)S(1)} collective-permute-done((bf16[8,32,256]{2,1,0:T(8,128)(2,1)S(1)}, bf16[8,32,256]{2,1,0:T(8,128)(2,1)S(1)}, u32[]{:S(2)}, u32[]{:S(2)}) %collective-permute-start.9) | collective-permute-done | bytes 131104 | tf_op jit(solution)/shard_map/ppermute | solution.py:34
  158.9 52.3 %all_to_all.32 = bf16[8,72,256]{2,1,0:T(8,128)(2,1)S(1)} all-to-all(bf16[8,72,256]{2,1,0:T(8,128)(2,1)S(1)} %pad_maximum_fusion.1), channel_id=1, replica_groups=mesh['za'=2,'zb'=4,'x'=4,'c'=2,'zh'=4,'y'=4] {'za','zh'}, dimensions={0} | all-to-all | bytes 589824 | tf_op jit(solution)/shard_map/all_to_all | solution.py:29
  (52 shorter events, 8.2 us)
Async XLA Ops:
  63.7 32.5 %all-to-all-start.1 = ((bf16[16,16,1024]{2,1,0:T(8,128)(2,1)}), bf16[16,16,1024]{2,1,0:T(8,128)(2,1)S(1)}, u32[]{:S(2)}, u32[]{:S(2)}) async-start(bf16[16,16,1024]{2,1,0:T(8,128)(2,1)} %bitcast.7), calls=%async_computation.1 | async-start | bytes 1048576 | tf_op jit(solution)/shard_map/all_to_all | solution.py:29
  76.0 8.6 %collective-permute-start = (bf16[8,32,256]{2,1,0:T(8,128)(2,1)S(1)}, bf16[8,32,256]{2,1,0:T(8,128)(2,1)S(1)}, u32[]{:S(2)}, u32[]{:S(2)}) collective-permute-start(bf16[8,32,256]{2,1,0:T(8,128)(2,1)S(1)} %get-tuple-element.30.refs_0_), channel_id=1, source_target_pairs={{0,32},{32,64},{64,96},{96,0},{1,33},{33,65},{65,97},{97,1},{2,34}... | collective-permute-start | bytes 393224 | tf_op jit(solution)/shard_map/ppermute | solution.py:34
  78.4 9.0 %collective-permute-start.1 = (bf16[8,32,256]{2,1,0:T(8,128)(2,1)S(1)}, bf16[8,32,256]{2,1,0:T(8,128)(2,1)S(1)}, u32[]{:S(2)}, u32[]{:S(2)}) collective-permute-start(bf16[8,32,256]{2,1,0:T(8,128)(2,1)S(1)} %get-tuple-element.30.refs_0_), channel_id=1, source_target_pairs={{0,64},{32,96},{64,0},{96,32},{1,65},{33,97},{65,1},{97,33},{2,66}... | collective-permute-start | bytes 393224 | tf_op jit(solution)/shard_map/ppermute | solution.py:34
  82.7 8.1 %collective-permute-start.2 = (bf16[8,32,256]{2,1,0:T(8,128)(2,1)S(1)}, bf16[8,32,256]{2,1,0:T(8,128)(2,1)S(1)}, u32[]{:S(2)}, u32[]{:S(2)}) collective-permute-start(bf16[8,32,256]{2,1,0:T(8,128)(2,1)S(1)} %get-tuple-element.30.refs_0_), channel_id=1, source_target_pairs={{0,96},{32,0},{64,32},{96,64},{1,97},{33,1},{65,33},{97,65},{2,98}... | collective-permute-start | bytes 393224 | tf_op jit(solution)/shard_map/ppermute | solution.py:34
  90.9 5.3 %collective-permute-start.3 = (bf16[3,8,32,256]{3,2,1,0:T(8,128)(2,1)S(1)}, bf16[3,8,32,256]{3,2,1,0:T(8,128)(2,1)S(1)}, u32[]{:S(2)}, u32[]{:S(2)}) collective-permute-start(bf16[3,8,32,256]{3,2,1,0:T(8,128)(2,1)S(1)} %pad_maximum_fusion), channel_id=1, source_target_pairs={{0,16},{16,0},{1,17},{17,1},{2,18},{18,2},{3,19},{19,3},{4,20},{20... | collective-permute-start | bytes 1179656 | tf_op jit(solution)/shard_map/ppermute | solution.py:34
  92.8 3.4 %collective-permute-start.4 = (bf16[8,32,256]{2,1,0:T(8,128)(2,1)S(1)}, bf16[8,32,256]{2,1,0:T(8,128)(2,1)S(1)}, u32[]{:S(2)}, u32[]{:S(2)}) collective-permute-start(bf16[8,32,256]{2,1,0:T(8,128)(2,1)S(1)} %get-tuple-element.30.refs_0_), channel_id=1, source_target_pairs={{0,16},{16,0},{1,17},{17,1},{2,18},{18,2},{3,19},{19,3},{4,20},{20... | collective-permute-start | bytes 393224 | tf_op jit(solution)/shard_map/ppermute | solution.py:34
  98.0 17.5 %all-to-all-start.2 = ((f32[32,16,256]{2,1,0:T(8,128)}), f32[32,16,256]{2,1,0:T(8,128)S(1)}, u32[]{:S(2)}, u32[]{:S(2)}) async-start(f32[32,16,256]{2,1,0:T(8,128)} %bitcast.9), calls=%async_computation.2 | async-start | bytes 1048576 | tf_op jit(solution)/shard_map/all_to_all | solution.py:29
  105.2 0.7 copy-start
  105.2 0.7 copy-start.1
  106.0 9.5 %collective-permute-start.5 = (s32[16,5]{1,0:T(8,128)S(1)}, s32[16,5]{1,0:T(8,128)S(1)}, u32[]{:S(2)}, u32[]{:S(2)}) collective-permute-start(s32[16,5]{1,0:T(8,128)S(1)} %copy.32), channel_id=1, source_target_pairs={{0,512},{512,0},{1,513},{513,1},{2,514},{514,2},{3,515},{515,3},{4... | collective-permute-start | bytes 968 | tf_op jit(solution)/shard_map/ppermute | solution.py:34
  131.2 27.0 %all-to-all-start.4 = ((bf16[16,16,1152]{2,1,0:T(8,128)(2,1)}), bf16[16,16,1152]{2,1,0:T(8,128)(2,1)S(1)}, u32[]{:S(2)}, u32[]{:S(2)}) async-start(bf16[16,16,1152]{2,1,0:T(8,128)(2,1)} %bitcast.18), calls=%async_computation.4 | async-start | bytes 1179648 | tf_op jit(solution)/shard_map/all_to_all | solution.py:29
  138.8 3.8 %collective-permute-start.6 = (bf16[4,8,32,256]{3,2,1,0:T(8,128)(2,1)S(1)}, bf16[4,8,32,256]{3,2,1,0:T(8,128)(2,1)S(1)}, u32[]{:S(2)}, u32[]{:S(2)}) collective-permute-start(bf16[4,8,32,256]{3,2,1,0:T(8,128)(2,1)S(1)} %slice_bitcast_fusion), channel_id=1, source_target_pairs={{0,16},{16,0},{1,17},{17,1},{2,18},{18,2},{3,19},{19,3},{4,20},{20... | collective-permute-start | bytes 1572872 | tf_op jit(solution)/shard_map/ppermute | solution.py:34
  142.8 9.3 %collective-permute-start.7 = (bf16[8,32,256]{2,1,0:T(8,128)(2,1)S(1)}, bf16[8,32,256]{2,1,0:T(8,128)(2,1)S(1)}, u32[]{:S(2)}, u32[]{:S(2)}) collective-permute-start(bf16[8,32,256]{2,1,0:T(8,128)(2,1)S(1)} %get-tuple-element.27), channel_id=1, source_target_pairs={{0,32},{32,64},{64,96},{96,0},{1,33},{33,65},{65,97},{97,1},{2,34}... | collective-permute-start | bytes 393224 | tf_op jit(solution)/shard_map/ppermute | solution.py:34
  146.7 9.2 %collective-permute-start.8 = (bf16[8,32,256]{2,1,0:T(8,128)(2,1)S(1)}, bf16[8,32,256]{2,1,0:T(8,128)(2,1)S(1)}, u32[]{:S(2)}, u32[]{:S(2)}) collective-permute-start(bf16[8,32,256]{2,1,0:T(8,128)(2,1)S(1)} %get-tuple-element.26), channel_id=1, source_target_pairs={{0,64},{32,96},{64,0},{96,32},{1,65},{33,97},{65,1},{97,33},{2,66}... | collective-permute-start | bytes 393224 | tf_op jit(solution)/shard_map/ppermute | solution.py:34
  149.4 8.8 %collective-permute-start.9 = (bf16[8,32,256]{2,1,0:T(8,128)(2,1)S(1)}, bf16[8,32,256]{2,1,0:T(8,128)(2,1)S(1)}, u32[]{:S(2)}, u32[]{:S(2)}) collective-permute-start(bf16[8,32,256]{2,1,0:T(8,128)(2,1)S(1)} %get-tuple-element.25), channel_id=1, source_target_pairs={{0,96},{32,0},{64,32},{96,64},{1,97},{33,1},{65,33},{97,65},{2,98}... | collective-permute-start | bytes 393224 | tf_op jit(solution)/shard_map/ppermute | solution.py:34

commit v4 on v3

v4 whole, which is shorter than its diff:
```python
import math

import jax
import jax.numpy as jnp
from jax import lax
from jax.experimental import pallas as pl
from jax.experimental.pallas import tpu as pltpu
from jax.sharding import Mesh, PartitionSpec as P

D = 4096
SIZES = {"za": 2, "zb": 4, "x": 4, "c": 2, "zh": 4, "y": 4}
ZA, ZB, X, C, ZH, Y = SIZES.values()
FAR = ("za", "zh")
A = ZA * ZH
NEAR = ("zb", "y")
PLANE = ("x", "y")
LANES = 128
hard_weight = 4.0
logit_scale = 4.0 / math.sqrt(D)
bf16, f32 = jnp.bfloat16, jnp.float32
params = pltpu.CompilerParams(vmem_limit_bytes=40 * 2**20)
whole = pl.BlockSpec(memory_space=pltpu.VMEM)
scalars = pl.BlockSpec(memory_space=pltpu.SMEM)


def exchange(x, axes):
    return lax.all_to_all(x, axes, 0, 0, tiled=True)


def shift(x, axis, by):
    n = SIZES[axis]
    return lax.ppermute(x, axis, [(i, (i + by) % n) for i in range(n)])


def logits_kernel(at_ref, *refs):
    q_refs, (p_ref, far_ref, out_ref, rows_ref) = refs[:X], refs[X:]
    n, k = q_refs[0].shape[1:]
    np_ = p_ref.shape[0]
    for j in range(X):
        g = lax.rem(at_ref[0] + X - j, X)
        for za in range(ZA):
            row = pl.multiple_of(g * (ZA * n) + za * n, n)
            for s in range(ZH):
                rows_ref[pl.ds(row, n), s * k : (s + 1) * k] = q_refs[j][za * ZH + s]
    for cc, ref in enumerate((p_ref, far_ref)):
        out_ref[:, cc * np_ : (cc + 1) * np_] = lax.dot_general(
            rows_ref[...], ref[...], (((1,), (1,)), ((), ())), preferred_element_type=f32
        )


def softmax_kernel(at_ref, part_ref, ids_ref, ds_ref, side_ref):
    rows, n = part_ref.shape[1:]
    positive = ids_ref[:, 0:1]
    col = lax.broadcasted_iota(jnp.int32, (rows, n), 1)
    base = (
        (((col >> 3) & 1) << 10)
        + (((col >> 6) & 3) << 8)
        + (((col >> 8) & 1) << 5)
        + (((col >> 1) & 3) << 3)
        + (((col >> 4) & 3) << 1)
        + (col & 1)
    ) ^ (at_ref[1] * 32)
    logits, top = [], None
    for g in range(X):
        a = part_ref[g * Y]
        for y in range(1, Y):
            a = a + part_ref[g * Y + y]
        a = a * logit_scale
        logits.append(a)
        m = jnp.max(a, axis=1, keepdims=True)
        top = m if top is None else jnp.maximum(top, m)
    total = jnp.zeros((rows, 1), f32)
    pos_logit = jnp.zeros((rows, 1), f32)
    scaled, hot = [], []
    for g in range(X):
        ids = base + g * 64
        onehot = ids == positive
        hard = ids == ids_ref[:, 1:2]
        for h in range(2, ids_ref.shape[1]):
            hard = jnp.logical_or(hard, ids == ids_ref[:, h : h + 1])
        hard = jnp.logical_and(hard, jnp.logical_not(onehot))
        e = jnp.where(hard, hard_weight, 1.0) * jnp.exp(logits[g] - top)
        total = total + jnp.sum(e, axis=1, keepdims=True)
        pos_logit = pos_logit + jnp.sum(jnp.where(onehot, logits[g], 0.0), axis=1, keepdims=True)
        scaled.append(e)
        hot.append(jnp.where(onehot, 1.0, 0.0))
    loss = top + jnp.log(total) - pos_logit
    hi = loss.astype(bf16).astype(f32)
    mid = (loss - hi).astype(bf16).astype(f32)
    lo = loss - hi - mid
    lane = lax.broadcasted_iota(jnp.int32, (rows, LANES), 1)
    side = jnp.where(lane == 0, hi, jnp.where(lane == 1, mid, jnp.where(lane == 2, lo, 0.0)))
    side_ref[...] = side
    for g in range(X):
        ds = (logit_scale * (scaled[g] / total - hot[g])).astype(bf16)
        for y in range(Y):
            ds_ref[g * Y + y] = ds


def grads_kernel(at_ref, ds_ref, side_ref, rows_ref, p_ref, far_ref, qg_ref, pg_ref, away_ref):
    n, k = qg_ref.shape[2:]
    np_, width = p_ref.shape
    away_ref[...] = lax.dot_general(
        ds_ref[:, np_:], rows_ref[...], (((0,), (0,)), ((), ())), preferred_element_type=f32
    ).astype(bf16)
    pg_ref[:, :width] = lax.dot_general(
        ds_ref[:, :np_], rows_ref[...], (((0,), (0,)), ((), ())), preferred_element_type=f32
    )
    nrow = side_ref.shape[0]
    for b in range(np_ // nrow):
        pg_ref[b * nrow : (b + 1) * nrow, width:] = side_ref[...]
    for j in range(X):
        row = pl.multiple_of(lax.rem(at_ref[0] + j, X) * (ZA * n), ZA * n)
        ds = ds_ref[pl.ds(row, ZA * n), :]
        terms = jnp.dot(ds[:, :np_], p_ref[...], preferred_element_type=f32)
        terms = terms + jnp.dot(ds[:, np_:], far_ref[...], preferred_element_type=f32)
        terms = terms.astype(bf16)
        for za in range(ZA):
            for s in range(ZH):
                qg_ref[j, za * ZH + s] = terms[za * n : (za + 1) * n, s * k : (s + 1) * k]


def on_device(queries, passages, positive, hard_negs):
    nq, k = queries.shape
    own, d = passages.shape
    n = nq // A
    nrow = ZA * n // Y
    width = ZH * k
    za, zh, y = lax.axis_index("za"), lax.axis_index("zh"), lax.axis_index("y")
    at = jnp.stack([lax.axis_index("x"), lax.axis_index("c")]).astype(jnp.int32)

    ids = jnp.concatenate([positive[:, None], hard_negs], axis=1)
    half = lax.rem(y, 2) * nrow
    mine = lax.dynamic_slice_in_dim(ids, (za * ZH + zh) * n + half, nrow, 0)
    other = lax.dynamic_slice_in_dim(ids, ((1 - za) * ZH + zh) * n + half, nrow, 0)
    other = shift(other, "za", 1)

    prow = own * d // k
    send = jnp.concatenate(
        [
            queries.astype(bf16).reshape(A, n, k),
            jnp.broadcast_to(passages.astype(bf16).reshape(1, prow, k), (A, prow, k)),
        ],
        axis=1,
    )
    got, other = lax.optimization_barrier((exchange(send, FAR), other))
    ids = jnp.where(y // 2 == za, mine, other)
    q = got[:, :n]
    qs = [q] + [shift(q, "x", j) for j in range(1, X)]

    few = A * own
    p = got[:, n:].reshape(A, own, ZH, Y, k).transpose(3, 0, 1, 2, 4).reshape(Y, few, width)
    p = jnp.broadcast_to(p[None], (ZB,) + p.shape).reshape(ZB * Y, few, width)
    qs, p = lax.optimization_barrier((qs, exchange(p, NEAR)))
    p = p.reshape(ZB * Y * few, width)
    far = shift(p, "c", 1)
    np_ = C * p.shape[0]

    parts, rows = pl.pallas_call(
        logits_kernel,
        in_specs=[scalars] + [whole] * (X + 2),
        out_specs=(whole, whole),
        out_shape=(
            jax.ShapeDtypeStruct((X * ZA * n, np_), f32),
            jax.ShapeDtypeStruct((X * ZA * n, width), bf16),
        ),
        compiler_params=params,
        name="logits",
    )(at, *qs, p, far)
    parts = exchange(parts.reshape(X * Y, nrow, np_), PLANE)

    ds, side = pl.pallas_call(
        softmax_kernel,
        in_specs=[scalars, whole, whole],
        out_specs=(whole, whole),
        out_shape=(
            jax.ShapeDtypeStruct((X * Y, nrow, np_), bf16),
            jax.ShapeDtypeStruct((nrow, LANES), f32),
        ),
        compiler_params=params,
        name="softmax",
    )(at, parts, ids)
    ds = exchange(ds, PLANE).reshape(X * ZA * n, np_)

    qg, pg, away = pl.pallas_call(
        grads_kernel,
        in_specs=[scalars] + [whole] * 5,
        out_specs=(whole, whole, whole),
        out_shape=(
            jax.ShapeDtypeStruct((X, A, n, k), bf16),
            jax.ShapeDtypeStruct((np_ // C, width + LANES), f32),
            jax.ShapeDtypeStruct((np_ // C, width), bf16),
        ),
        compiler_params=params,
        name="grads",
    )(at, ds, side, rows, p, far)

    away = jnp.pad(shift(away, "c", 1), ((0, 0), (0, LANES)))
    pg = (pg + away.astype(f32)).astype(bf16).reshape(ZB * Y, few, width + LANES)
    pg = exchange(pg, NEAR)
    terms = [qg[0]] + [shift(qg[j], "x", j) for j in range(1, X)]
    terms, pg = lax.optimization_barrier((terms, pg))
    qg = sum(t.astype(f32) for t in terms).astype(bf16)
    side = lax.dynamic_slice_in_dim(pg, lax.axis_index("zb") * Y, Y, 0)[:, :, width : width + 3]
    pg = jnp.sum(pg[:, :, :width].astype(f32).reshape(ZB, Y, few, width), axis=0)
    pg = pg.astype(bf16).reshape(Y, A, own, ZH, k).transpose(1, 2, 3, 0, 4).reshape(A, prow, k)

    loss = side.reshape(ZA, n, 3).transpose(0, 2, 1).reshape(ZA, 1, 3 * n)
    loss = jnp.pad(loss, ((0, 0), (0, 7), (0, k - 3 * n)))
    loss = jnp.broadcast_to(loss[:, None], (ZA, ZH, 8, k)).reshape(A, 8, k)
    got = exchange(jnp.concatenate([qg, pg, loss], axis=1), FAR)
    qg = got[:, :n].reshape(nq, k).astype(f32)
    pg = jnp.sum(got[:, n : n + prow].astype(f32), axis=0).reshape(own, d)
    loss = got[:, n + prow, : 3 * n].astype(f32).reshape(A, 3, n)
    row_loss = (loss[:, 0] + loss[:, 1] + loss[:, 2]).reshape(nq)
    return row_loss, qg, pg


def solution(mesh):
    fine = Mesh(mesh.devices.reshape(*SIZES.values()), tuple(SIZES))
    dp, sub = ("za", "zb", "x", "c"), ("zh", "y")
    return jax.shard_map(
        on_device,
        mesh=fine,
        in_specs=(P(dp, sub), P(dp + sub, None), P(dp), P(dp, None)),
        out_specs=(P(dp), P(dp, sub), P(dp + sub, None)),
        check_vma=False,
    )
```

time: 214 us -> 211 us (0.986)
  the two profiles are of different devices: /device:TPU:14 before, /device:TPU:32 now
where the time goes in v4:
time: 211 us; the launch traced here: 210 us
  starting transfers between devices  78.6 us (37%)
  blocking collectives  62.1 us (29%)
  waiting for transfers between devices  56.7 us (27%)
  other arithmetic  4.57 us (2%)
  Pallas kernels  4.38 us (2%)
  local copies, waits for them, and re-layouts  3.13 us (1%)
    all_to_all x2, blocking collectives, exchange(): return lax.all_to_all(x, axes, 0, 0, tiled=True)  62.1 us
    all_to_all x4, starting transfers between devices, exchange(): return lax.all_to_all(x, axes, 0, 0, tiled=True)  45.9 us
    ppermute x9, starting transfers between devices, shift(): return lax.ppermute(x, axis, [(i, (i + by) % n) for i in range(n)])  32.7 us
    all_to_all x4, waiting for transfers between devices, exchange(): return lax.all_to_all(x, axes, 0, 0, tiled=True)  30.4 us
    ppermute x9, waiting for transfers between devices, shift(): return lax.ppermute(x, axis, [(i, (i + by) % n) for i in range(n)])  26.3 us
  transfers between devices with their start and end apart: 13, of which 10 were waited for; matrix products, arithmetic and copies ran while one was open for 0% of the time, Pallas kernels for 0%

profile of v4, /device:TPU:32, one launch (start us, length us, event | category | flops | bytes accessed | tf_op | source)
XLA Modules:
  0.0 210.4 jit_solution(5167704954835192382)
XLA Ops:
  3.2 27.4 %all-to-all-start = ((bf16[8,64,256]{2,1,0:T(8,128)(2,1)}), bf16[8,64,256]{2,1,0:T(8,128)(2,1)S(1)}, u32[]{:S(2)}, u32[]{:S(2)}) async-start(bf16[8,64,256]{2,1,0:T(8,128)(2,1)} %pad_maximum_fusion.1), calls=%async_computation | async-start | bytes 524288 | tf_op jit(solution)/shard_map/all_to_all | solution.py:27
  30.8 7.8 %collective-permute-start = (s32[16,5]{1,0:T(8,128)S(1)}, s32[16,5]{1,0:T(8,128)S(1)}, u32[]{:S(2)}, u32[]{:S(2)}) collective-permute-start(s32[16,5]{1,0:T(8,128)S(1)} %copy.31), channel_id=1, source_target_pairs={{0,512},{512,0},{1,513},{513,1},{2,514},{514,2},{3,515},{515,3},{4... | collective-permute-start | bytes 968 | tf_op jit(solution)/shard_map/ppermute | solution.py:32
  38.6 15.2 %collective-permute-done = s32[16,5]{1,0:T(8,128)S(1)} collective-permute-done((s32[16,5]{1,0:T(8,128)S(1)}, s32[16,5]{1,0:T(8,128)S(1)}, u32[]{:S(2)}, u32[]{:S(2)}) %collective-permute-start) | collective-permute-done | bytes 352 | tf_op jit(solution)/shard_map/ppermute | solution.py:32
  53.8 15.9 %all-to-all-done = bf16[8,64,256]{2,1,0:T(8,128)(2,1)S(1)} async-done(((bf16[8,64,256]{2,1,0:T(8,128)(2,1)}), bf16[8,64,256]{2,1,0:T(8,128)(2,1)S(1)}, u32[]{:S(2)}, u32[]{:S(2)}) %all-to-all-start) | async-done | bytes 262176 | tf_op jit(solution)/shard_map/all_to_all | solution.py:27
  70.8 5.9 %all-to-all-start.1 = ((bf16[16,16,1024]{2,1,0:T(8,128)(2,1)}), bf16[16,16,1024]{2,1,0:T(8,128)(2,1)S(1)}, u32[]{:S(2)}, u32[]{:S(2)}) async-start(bf16[16,16,1024]{2,1,0:T(8,128)(2,1)} %bitcast.5), calls=%async_computation.1 | async-start | bytes 1048576 | tf_op jit(solution)/shard_map/all_to_all | solution.py:27
  76.8 3.4 %collective-permute-start.1 = (bf16[8,32,256]{2,1,0:T(8,128)(2,1)S(1)}, bf16[8,32,256]{2,1,0:T(8,128)(2,1)S(1)}, u32[]{:S(2)}, u32[]{:S(2)}) collective-permute-start(bf16[8,32,256]{2,1,0:T(8,128)(2,1)S(1)} %get-tuple-element.23.refs_0_), channel_id=1, source_target_pairs={{0,32},{32,64},{64,96},{96,0},{1,33},{33,65},{65,97},{97,1},{2,34}... | collective-permute-start | bytes 393224 | tf_op jit(solution)/shard_map/ppermute | solution.py:32
  80.2 4.6 %collective-permute-start.2 = (bf16[8,32,256]{2,1,0:T(8,128)(2,1)S(1)}, bf16[8,32,256]{2,1,0:T(8,128)(2,1)S(1)}, u32[]{:S(2)}, u32[]{:S(2)}) collective-permute-start(bf16[8,32,256]{2,1,0:T(8,128)(2,1)S(1)} %get-tuple-element.23.refs_0_), channel_id=1, source_target_pairs={{0,64},{32,96},{64,0},{96,32},{1,65},{33,97},{65,1},{97,33},{2,66}... | collective-permute-start | bytes 393224 | tf_op jit(solution)/shard_map/ppermute | solution.py:32
  84.8 3.3 %collective-permute-start.3 = (bf16[8,32,256]{2,1,0:T(8,128)(2,1)S(1)}, bf16[8,32,256]{2,1,0:T(8,128)(2,1)S(1)}, u32[]{:S(2)}, u32[]{:S(2)}) collective-permute-start(bf16[8,32,256]{2,1,0:T(8,128)(2,1)S(1)} %get-tuple-element.23.refs_0_), channel_id=1, source_target_pairs={{0,96},{32,0},{64,32},{96,64},{1,97},{33,1},{65,33},{97,65},{2,98}... | collective-permute-start | bytes 393224 | tf_op jit(solution)/shard_map/ppermute | solution.py:32
  88.5 3.1 %collective-permute-done.3.refs_3_ = bf16[8,32,256]{2,1,0:T(8,128)(2,1)S(1)} collective-permute-done((bf16[8,32,256]{2,1,0:T(8,128)(2,1)S(1)}, bf16[8,32,256]{2,1,0:T(8,128)(2,1)S(1)}, u32[]{:S(2)}, u32[]{:S(2)}) %collective-permute-start.3) | collective-permute-done | bytes 131104 | tf_op jit(solution)/shard_map/ppermute | solution.py:32
  91.7 1.9 collective-permute-start.4
  93.7 1.8 collective-permute-done.4.refs_5_.far_ref
  95.5 1.8 logits.1
  97.3 6.4 %all-to-all-start.2 = ((f32[16,16,512]{2,1,0:T(8,128)}), f32[16,16,512]{2,1,0:T(8,128)S(1)}, u32[]{:S(2)}, u32[]{:S(2)}) async-start(f32[16,16,512]{2,1,0:T(8,128)} %bitcast.7), calls=%async_computation.2 | async-start | bytes 1048576 | tf_op jit(solution)/shard_map/all_to_all | solution.py:27
  103.8 11.7 %all-to-all-done.2.part_ref = f32[16,16,512]{2,1,0:T(8,128)S(1)} async-done(((f32[16,16,512]{2,1,0:T(8,128)}), f32[16,16,512]{2,1,0:T(8,128)S(1)}, u32[]{:S(2)}, u32[]{:S(2)}) %all-to-all-start.2) | async-done | bytes 524320 | tf_op jit(solution)/shard_map/all_to_all | solution.py:27
  116.4 11.7 %all_to_all.30 = bf16[16,16,512]{2,1,0:T(8,128)(2,1)S(1)} all-to-all(bf16[16,16,512]{2,1,0:T(8,128)(2,1)S(1)} %get-tuple-element.30), channel_id=1, replica_groups=mesh['za'=2,'zb'=4,'x'=4,'c'=2,'zh'=4,'y'=4] {'x','y'}, dimensions={0} | all-to-all | bytes 524288 | tf_op jit(solution)/shard_map/all_to_all | solution.py:27
  129.8 1.9 collective-permute-start.8
  131.7 1.9 collective-permute-done.8
  134.6 6.1 %all-to-all-start.4 = ((bf16[16,16,1152]{2,1,0:T(8,128)(2,1)}), bf16[16,16,1152]{2,1,0:T(8,128)(2,1)S(1)}, u32[]{:S(2)}, u32[]{:S(2)}) async-start(bf16[16,16,1152]{2,1,0:T(8,128)(2,1)} %bitcast.13), calls=%async_computation.4 | async-start | bytes 1179648 | tf_op jit(solution)/shard_map/all_to_all | solution.py:27
  140.7 2.3 %collective-permute-start.5 = (bf16[8,32,256]{2,1,0:T(8,128)(2,1)S(1)}, bf16[8,32,256]{2,1,0:T(8,128)(2,1)S(1)}, u32[]{:S(2)}, u32[]{:S(2)}) collective-permute-start(bf16[8,32,256]{2,1,0:T(8,128)(2,1)S(1)} %get-tuple-element.43), channel_id=1, source_target_pairs={{0,32},{32,64},{64,96},{96,0},{1,33},{33,65},{65,97},{97,1},{2,34}... | collective-permute-start | bytes 393224 | tf_op jit(solution)/shard_map/ppermute | solution.py:32
  143.0 4.0 %collective-permute-start.6 = (bf16[8,32,256]{2,1,0:T(8,128)(2,1)S(1)}, bf16[8,32,256]{2,1,0:T(8,128)(2,1)S(1)}, u32[]{:S(2)}, u32[]{:S(2)}) collective-permute-start(bf16[8,32,256]{2,1,0:T(8,128)(2,1)S(1)} %get-tuple-element.42), channel_id=1, source_target_pairs={{0,64},{32,96},{64,0},{96,32},{1,65},{33,97},{65,1},{97,33},{2,66}... | collective-permute-start | bytes 393224 | tf_op jit(solution)/shard_map/ppermute | solution.py:32
  147.0 3.4 %collective-permute-start.7 = (bf16[8,32,256]{2,1,0:T(8,128)(2,1)S(1)}, bf16[8,32,256]{2,1,0:T(8,128)(2,1)S(1)}, u32[]{:S(2)}, u32[]{:S(2)}) collective-permute-start(bf16[8,32,256]{2,1,0:T(8,128)(2,1)S(1)} %get-tuple-element.41), channel_id=1, source_target_pairs={{0,96},{32,0},{64,32},{96,64},{1,97},{33,1},{65,33},{97,65},{2,98}... | collective-permute-start | bytes 393224 | tf_op jit(solution)/shard_map/ppermute | solution.py:32
  151.6 2.8 %collective-permute-done.7 = bf16[8,32,256]{2,1,0:T(8,128)(2,1)S(1)} collective-permute-done((bf16[8,32,256]{2,1,0:T(8,128)(2,1)S(1)}, bf16[8,32,256]{2,1,0:T(8,128)(2,1)S(1)}, u32[]{:S(2)}, u32[]{:S(2)}) %collective-permute-start.7) | collective-permute-done | bytes 131104 | tf_op jit(solution)/shard_map/ppermute | solution.py:32
  154.3 2.8 %all-to-all-done.4 = bf16[16,16,1152]{2,1,0:T(8,128)(2,1)S(1)} async-done(((bf16[16,16,1152]{2,1,0:T(8,128)(2,1)}), bf16[16,16,1152]{2,1,0:T(8,128)(2,1)S(1)}, u32[]{:S(2)}, u32[]{:S(2)}) %all-to-all-start.4) | async-done | bytes 589856 | tf_op jit(solution)/shard_map/all_to_all | solution.py:27
  157.8 50.4 %all_to_all.31 = bf16[8,72,256]{2,1,0:T(8,128)(2,1)S(1)} all-to-all(bf16[8,72,256]{2,1,0:T(8,128)(2,1)S(1)} %pad_maximum_fusion), channel_id=1, replica_groups=mesh['za'=2,'zb'=4,'x'=4,'c'=2,'zh'=4,'y'=4] {'za','zh'}, dimensions={0} | all-to-all | bytes 589824 | tf_op jit(solution)/shard_map/all_to_all | solution.py:27
  (49 shorter events, 11.8 us)
Async XLA Ops:
  0.6 30.0 %copy-start.1 = (s32[256]{0:T(256)S(1)}, s32[256]{0:T(256)}, u32[]{:S(2)}) copy-start(s32[256]{0:T(256)} %param.6) | copy-start | bytes 3076
  0.6 30.0 %copy-start = (s32[256,4]{0,1:T(4,128)S(1)}, s32[256,4]{0,1:T(4,128)}, u32[]{:S(2)}) copy-start(s32[256,4]{0,1:T(4,128)} %param.7) | copy-start | bytes 12292
  3.2 66.6 %all-to-all-start = ((bf16[8,64,256]{2,1,0:T(8,128)(2,1)}), bf16[8,64,256]{2,1,0:T(8,128)(2,1)S(1)}, u32[]{:S(2)}, u32[]{:S(2)}) async-start(bf16[8,64,256]{2,1,0:T(8,128)(2,1)} %pad_maximum_fusion.1), calls=%async_computation | async-start | bytes 524288 | tf_op jit(solution)/shard_map/all_to_all | solution.py:27
  30.8 23.0 %collective-permute-start = (s32[16,5]{1,0:T(8,128)S(1)}, s32[16,5]{1,0:T(8,128)S(1)}, u32[]{:S(2)}, u32[]{:S(2)}) collective-permute-start(s32[16,5]{1,0:T(8,128)S(1)} %copy.31), channel_id=1, source_target_pairs={{0,512},{512,0},{1,513},{513,1},{2,514},{514,2},{3,515},{515,3},{4... | collective-permute-start | bytes 968 | tf_op jit(solution)/shard_map/ppermute | solution.py:32
  70.8 20.9 %all-to-all-start.1 = ((bf16[16,16,1024]{2,1,0:T(8,128)(2,1)}), bf16[16,16,1024]{2,1,0:T(8,128)(2,1)S(1)}, u32[]{:S(2)}, u32[]{:S(2)}) async-start(bf16[16,16,1024]{2,1,0:T(8,128)(2,1)} %bitcast.5), calls=%async_computation.1 | async-start | bytes 1048576 | tf_op jit(solution)/shard_map/all_to_all | solution.py:27
  76.8 11.4 %collective-permute-start.1 = (bf16[8,32,256]{2,1,0:T(8,128)(2,1)S(1)}, bf16[8,32,256]{2,1,0:T(8,128)(2,1)S(1)}, u32[]{:S(2)}, u32[]{:S(2)}) collective-permute-start(bf16[8,32,256]{2,1,0:T(8,128)(2,1)S(1)} %get-tuple-element.23.refs_0_), channel_id=1, source_target_pairs={{0,32},{32,64},{64,96},{96,0},{1,33},{33,65},{65,97},{97,1},{2,34}... | collective-permute-start | bytes 393224 | tf_op jit(solution)/shard_map/ppermute | solution.py:32
  80.2 8.4 %collective-permute-start.2 = (bf16[8,32,256]{2,1,0:T(8,128)(2,1)S(1)}, bf16[8,32,256]{2,1,0:T(8,128)(2,1)S(1)}, u32[]{:S(2)}, u32[]{:S(2)}) collective-permute-start(bf16[8,32,256]{2,1,0:T(8,128)(2,1)S(1)} %get-tuple-element.23.refs_0_), channel_id=1, source_target_pairs={{0,64},{32,96},{64,0},{96,32},{1,65},{33,97},{65,1},{97,33},{2,66}... | collective-permute-start | bytes 393224 | tf_op jit(solution)/shard_map/ppermute | solution.py:32
  84.8 6.9 %collective-permute-start.3 = (bf16[8,32,256]{2,1,0:T(8,128)(2,1)S(1)}, bf16[8,32,256]{2,1,0:T(8,128)(2,1)S(1)}, u32[]{:S(2)}, u32[]{:S(2)}) collective-permute-start(bf16[8,32,256]{2,1,0:T(8,128)(2,1)S(1)} %get-tuple-element.23.refs_0_), channel_id=1, source_target_pairs={{0,96},{32,0},{64,32},{96,64},{1,97},{33,1},{65,33},{97,65},{2,98}... | collective-permute-start | bytes 393224 | tf_op jit(solution)/shard_map/ppermute | solution.py:32
  91.7 3.8 %collective-permute-start.4 = (bf16[256,1024]{1,0:T(8,128)(2,1)S(1)}, bf16[256,1024]{1,0:T(8,128)(2,1)S(1)}, u32[]{:S(2)}, u32[]{:S(2)}) collective-permute-start(bf16[256,1024]{1,0:T(8,128)(2,1)S(1)} %bitcast.28), channel_id=1, source_target_pairs={{0,16},{16,0},{1,17},{17,1},{2,18},{18,2},{3,19},{19,3},{4,20},{20... | collective-permute-start | bytes 1572872 | tf_op jit(solution)/shard_map/ppermute | solution.py:32
  97.3 18.2 %all-to-all-start.2 = ((f32[16,16,512]{2,1,0:T(8,128)}), f32[16,16,512]{2,1,0:T(8,128)S(1)}, u32[]{:S(2)}, u32[]{:S(2)}) async-start(f32[16,16,512]{2,1,0:T(8,128)} %bitcast.7), calls=%async_computation.2 | async-start | bytes 1048576 | tf_op jit(solution)/shard_map/all_to_all | solution.py:27
  129.8 3.8 %collective-permute-start.8 = (bf16[256,1024]{1,0:T(8,128)(2,1)S(1)}, bf16[256,1024]{1,0:T(8,128)(2,1)S(1)}, u32[]{:S(2)}, u32[]{:S(2)}) collective-permute-start(bf16[256,1024]{1,0:T(8,128)(2,1)S(1)} %get-tuple-element.35), channel_id=1, source_target_pairs={{0,16},{16,0},{1,17},{17,1},{2,18},{18,2},{3,19},{19,3},{4,20},{20... | collective-permute-start | bytes 1572872 | tf_op jit(solution)/shard_map/ppermute | solution.py:32
  134.6 22.5 %all-to-all-start.4 = ((bf16[16,16,1152]{2,1,0:T(8,128)(2,1)}), bf16[16,16,1152]{2,1,0:T(8,128)(2,1)S(1)}, u32[]{:S(2)}, u32[]{:S(2)}) async-start(bf16[16,16,1152]{2,1,0:T(8,128)(2,1)} %bitcast.13), calls=%async_computation.4 | async-start | bytes 1179648 | tf_op jit(solution)/shard_map/all_to_all | solution.py:27
  140.7 10.9 %collective-permute-start.5 = (bf16[8,32,256]{2,1,0:T(8,128)(2,1)S(1)}, bf16[8,32,256]{2,1,0:T(8,128)(2,1)S(1)}, u32[]{:S(2)}, u32[]{:S(2)}) collective-permute-start(bf16[8,32,256]{2,1,0:T(8,128)(2,1)S(1)} %get-tuple-element.43), channel_id=1, source_target_pairs={{0,32},{32,64},{64,96},{96,0},{1,33},{33,65},{65,97},{97,1},{2,34}... | collective-permute-start | bytes 393224 | tf_op jit(solution)/shard_map/ppermute | solution.py:32
  143.0 8.6 %collective-permute-start.6 = (bf16[8,32,256]{2,1,0:T(8,128)(2,1)S(1)}, bf16[8,32,256]{2,1,0:T(8,128)(2,1)S(1)}, u32[]{:S(2)}, u32[]{:S(2)}) collective-permute-start(bf16[8,32,256]{2,1,0:T(8,128)(2,1)S(1)} %get-tuple-element.42), channel_id=1, source_target_pairs={{0,64},{32,96},{64,0},{96,32},{1,65},{33,97},{65,1},{97,33},{2,66}... | collective-permute-start | bytes 393224 | tf_op jit(solution)/shard_map/ppermute | solution.py:32
  147.0 7.4 %collective-permute-start.7 = (bf16[8,32,256]{2,1,0:T(8,128)(2,1)S(1)}, bf16[8,32,256]{2,1,0:T(8,128)(2,1)S(1)}, u32[]{:S(2)}, u32[]{:S(2)}) collective-permute-start(bf16[8,32,256]{2,1,0:T(8,128)(2,1)S(1)} %get-tuple-element.41), channel_id=1, source_target_pairs={{0,96},{32,0},{64,32},{96,64},{1,97},{33,1},{65,33},{97,65},{2,98}... | collective-permute-start | bytes 393224 | tf_op jit(solution)/shard_map/ppermute | solution.py:32

commit v5 on v4

--- a/solution.py
+++ b/solution.py
@@ -32,20 +32,40 @@
     return lax.ppermute(x, axis, [(i, (i + by) % n) for i in range(n)])
 
 
+def pack_kernel(q_ref, p_ref, out_ref, rows_ref):
+    groups, _, k = out_ref.shape
+    n = q_ref.shape[0] // groups
+    own, d = p_ref.shape
+    for r in range(own):
+        for t in range(d // k):
+            i = r * (d // k) + t
+            rows_ref[i : i + 1, :] = p_ref[r : r + 1, t * k : (t + 1) * k]
+    p = rows_ref[...].astype(bf16)
+    for g in range(groups):
+        out_ref[g, :n] = q_ref[g * n : (g + 1) * n, :].astype(bf16)
+        out_ref[g, n:] = p
+
+
 def logits_kernel(at_ref, *refs):
-    q_refs, (p_ref, far_ref, out_ref, rows_ref) = refs[:X], refs[X:]
+    q_refs, (p_ref, out_ref, rows_ref) = refs[:X], refs[X:]
     n, k = q_refs[0].shape[1:]
-    np_ = p_ref.shape[0]
     for j in range(X):
         g = lax.rem(at_ref[0] + X - j, X)
         for za in range(ZA):
             row = pl.multiple_of(g * (ZA * n) + za * n, n)
             for s in range(ZH):
                 rows_ref[pl.ds(row, n), s * k : (s + 1) * k] = q_refs[j][za * ZH + s]
-    for cc, ref in enumerate((p_ref, far_ref)):
-        out_ref[:, cc * np_ : (cc + 1) * np_] = lax.dot_general(
-            rows_ref[...], ref[...], (((1,), (1,)), ((), ())), preferred_element_type=f32
-        )
+    out_ref[...] = lax.dot_general(
+        rows_ref[...], p_ref[...], (((1,), (1,)), ((), ())), preferred_element_type=f32
+    )
+
+
+def more_logits_kernel(rows_ref, far_ref, near_ref, out_ref):
+    np_ = far_ref.shape[0]
+    out_ref[:, :np_] = near_ref[...]
+    out_ref[:, np_:] = lax.dot_general(
+        rows_ref[...], far_ref[...], (((1,), (1,)), ((), ())), preferred_element_type=f32
+    )
 
 
 def softmax_kernel(at_ref, part_ref, ids_ref, ds_ref, side_ref):
@@ -97,12 +117,16 @@
             ds_ref[g * Y + y] = ds
 
 
-def grads_kernel(at_ref, ds_ref, side_ref, rows_ref, p_ref, far_ref, qg_ref, pg_ref, away_ref):
-    n, k = qg_ref.shape[2:]
-    np_, width = p_ref.shape
+def away_kernel(ds_ref, rows_ref, away_ref):
+    np_ = away_ref.shape[0]
     away_ref[...] = lax.dot_general(
         ds_ref[:, np_:], rows_ref[...], (((0,), (0,)), ((), ())), preferred_element_type=f32
     ).astype(bf16)
+
+
+def grads_kernel(at_ref, ds_ref, side_ref, rows_ref, p_ref, far_ref, qg_ref, pg_ref):
+    n, k = qg_ref.shape[2:]
+    np_, width = p_ref.shape
     pg_ref[:, :width] = lax.dot_general(
         ds_ref[:, :np_], rows_ref[...], (((0,), (0,)), ((), ())), preferred_element_type=f32
     )
@@ -136,14 +160,14 @@
     other = shift(other, "za", 1)
 
     prow = own * d // k
-    send = jnp.concatenate(
-        [
-            queries.astype(bf16).reshape(A, n, k),
-            jnp.broadcast_to(passages.astype(bf16).reshape(1, prow, k), (A, prow, k)),
-        ],
-        axis=1,
-    )
-    got, other = lax.optimization_barrier((exchange(send, FAR), other))
+    send = pl.pallas_call(
+        pack_kernel,
+        out_shape=jax.ShapeDtypeStruct((A, n + prow, k), bf16),
+        scratch_shapes=[pltpu.VMEM((prow, k), f32)],
+        compiler_params=params,
+        name="pack",
+    )(queries, passages)
+    got = exchange(send, FAR)
     ids = jnp.where(y // 2 == za, mine, other)
     q = got[:, :n]
     qs = [q] + [shift(q, "x", j) for j in range(1, X)]
@@ -156,17 +180,23 @@
     far = shift(p, "c", 1)
     np_ = C * p.shape[0]
 
-    parts, rows = pl.pallas_call(
+    near, rows = pl.pallas_call(
         logits_kernel,
-        in_specs=[scalars] + [whole] * (X + 2),
+        in_specs=[scalars] + [whole] * (X + 1),
         out_specs=(whole, whole),
         out_shape=(
-            jax.ShapeDtypeStruct((X * ZA * n, np_), f32),
+            jax.ShapeDtypeStruct((X * ZA * n, np_ // C), f32),
             jax.ShapeDtypeStruct((X * ZA * n, width), bf16),
         ),
         compiler_params=params,
         name="logits",
-    )(at, *qs, p, far)
+    )(at, *qs, p)
+    parts = pl.pallas_call(
+        more_logits_kernel,
+        out_shape=jax.ShapeDtypeStruct((X * ZA * n, np_), f32),
+        compiler_params=params,
+        name="more_logits",
+    )(rows, far, near)
     parts = exchange(parts.reshape(X * Y, nrow, np_), PLANE)
 
     ds, side = pl.pallas_call(
@@ -182,20 +212,26 @@
     )(at, parts, ids)
     ds = exchange(ds, PLANE).reshape(X * ZA * n, np_)
 
-    qg, pg, away = pl.pallas_call(
+    away = pl.pallas_call(
+        away_kernel,
+        out_shape=jax.ShapeDtypeStruct((np_ // C, width), bf16),
+        compiler_params=params,
+        name="away",
+    )(ds, rows)
+    away = shift(away, "c", 1)
+    qg, pg = pl.pallas_call(
         grads_kernel,
         in_specs=[scalars] + [whole] * 5,
-        out_specs=(whole, whole, whole),
+        out_specs=(whole, whole),
         out_shape=(
             jax.ShapeDtypeStruct((X, A, n, k), bf16),
             jax.ShapeDtypeStruct((np_ // C, width + LANES), f32),
-            jax.ShapeDtypeStruct((np_ // C, width), bf16),
         ),
         compiler_params=params,
         name="grads",
     )(at, ds, side, rows, p, far)
 
-    away = jnp.pad(shift(away, "c", 1), ((0, 0), (0, LANES)))
+    away = jnp.pad(away, ((0, 0), (0, LANES)))
     pg = (pg + away.astype(f32)).astype(bf16).reshape(ZB * Y, few, width + LANES)
     pg = exchange(pg, NEAR)
     terms = [qg[0]] + [shift(qg[j], "x", j) for j in range(1, X)]

time: 211 us -> 210 us (level)
  blocking collectives: 62.1 us -> 130 us
  waiting for transfers between devices: 56.7 us -> 17.9 us
  starting transfers between devices: 78.6 us -> 48.4 us
  other arithmetic: 4.57 us -> 2.09 us
    all_to_all x2 -> x3, blocking collectives: 62.1 us -> 130 us  [exchange(): return lax.all_to_all(x, axes, 0, 0, tiled=True)]
    all_to_all x4 -> x3, starting transfers between devices: 45.9 us -> 18.4 us  [exchange(): return lax.all_to_all(x, axes, 0, 0, tiled=True)]
    all_to_all x4 -> x3, waiting for transfers between devices: 30.4 us -> 4.97 us  [exchange(): return lax.all_to_all(x, axes, 0, 0, tiled=True)]
    ppermute x9, waiting for transfers between devices: 26.3 us -> 13 us  [shift(): return lax.ppermute(x, axis, [(i, (i + by) % n) for i in range(n)])]
    ppermute x9, starting transfers between devices: 32.7 us -> 29.9 us  [shift(): return lax.ppermute(x, axis, [(i, (i + by) % n) for i in range(n)])]
  transfers between devices with their start and end apart: 13 -> 12, of which waited for: 10 -> 9; matrix products, arithmetic and copies ran while one was open for 0% -> 0% of each run, Pallas kernels for 0% -> 1%
where the time goes in v5:
time: 210 us; the launch traced here: 209 us
  blocking collectives  130 us (62%)
  starting transfers between devices  48.4 us (23%)
  waiting for transfers between devices  17.9 us (9%)
  local copies, waits for them, and re-layouts  4.8 us (2%)
  Pallas kernels  4.8 us (2%)
    all_to_all x3, blocking collectives, exchange(): return lax.all_to_all(x, axes, 0, 0, tiled=True)  130 us
    ppermute x9, starting transfers between devices, shift(): return lax.ppermute(x, axis, [(i, (i + by) % n) for i in range(n)])  29.9 us
    all_to_all x3, starting transfers between devices, exchange(): return lax.all_to_all(x, axes, 0, 0, tiled=True)  18.4 us
    ppermute x9, waiting for transfers between devices, shift(): return lax.ppermute(x, axis, [(i, (i + by) % n) for i in range(n)])  13 us
    all_to_all x3, waiting for transfers between devices, exchange(): return lax.all_to_all(x, axes, 0, 0, tiled=True)  4.97 us
  transfers between devices with their start and end apart: 12, of which 9 were waited for; matrix products, arithmetic and copies ran while one was open for 0% of the time, Pallas kernels for 1%

profile of v5, /device:TPU:32, one launch (start us, length us, event | category | flops | bytes accessed | tf_op | source)
XLA Modules:
  0.0 208.6 jit_solution(5442149673134217819)
XLA Ops:
  2.4 66.2 %all_to_all.30 = bf16[8,64,256]{2,1,0:T(8,128)(2,1)S(1)} all-to-all(bf16[8,64,256]{2,1,0:T(8,128)(2,1)S(1)} %pack.1), channel_id=1, replica_groups=mesh['za'=2,'zb'=4,'x'=4,'c'=2,'zh'=4,'y'=4] {'za','zh'}, dimensions={0} | all-to-all | bytes 524288 | tf_op jit(solution)/shard_map/all_to_all | solution.py:27
  69.7 5.9 %all-to-all-start.1 = ((bf16[16,16,1024]{2,1,0:T(8,128)(2,1)}), bf16[16,16,1024]{2,1,0:T(8,128)(2,1)S(1)}, u32[]{:S(2)}, u32[]{:S(2)}) async-start(bf16[16,16,1024]{2,1,0:T(8,128)(2,1)} %bitcast.3), calls=%async_computation.1 | async-start | bytes 1048576 | tf_op jit(solution)/shard_map/all_to_all | solution.py:27
  75.6 3.4 %collective-permute-start = (bf16[8,32,256]{2,1,0:T(8,128)(2,1)S(1)}, bf16[8,32,256]{2,1,0:T(8,128)(2,1)S(1)}, u32[]{:S(2)}, u32[]{:S(2)}) collective-permute-start(bf16[8,32,256]{2,1,0:T(8,128)(2,1)S(1)} %get-tuple-element.19.refs_0_), channel_id=1, source_target_pairs={{0,32},{32,64},{64,96},{96,0},{1,33},{33,65},{65,97},{97,1},{2,34}... | collective-permute-start | bytes 393224 | tf_op jit(solution)/shard_map/ppermute | solution.py:32
  79.0 4.6 %collective-permute-start.1 = (bf16[8,32,256]{2,1,0:T(8,128)(2,1)S(1)}, bf16[8,32,256]{2,1,0:T(8,128)(2,1)S(1)}, u32[]{:S(2)}, u32[]{:S(2)}) collective-permute-start(bf16[8,32,256]{2,1,0:T(8,128)(2,1)S(1)} %get-tuple-element.19.refs_0_), channel_id=1, source_target_pairs={{0,64},{32,96},{64,0},{96,32},{1,65},{33,97},{65,1},{97,33},{2,66}... | collective-permute-start | bytes 393224 | tf_op jit(solution)/shard_map/ppermute | solution.py:32
  83.7 3.3 %collective-permute-start.2 = (bf16[8,32,256]{2,1,0:T(8,128)(2,1)S(1)}, bf16[8,32,256]{2,1,0:T(8,128)(2,1)S(1)}, u32[]{:S(2)}, u32[]{:S(2)}) collective-permute-start(bf16[8,32,256]{2,1,0:T(8,128)(2,1)S(1)} %get-tuple-element.19.refs_0_), channel_id=1, source_target_pairs={{0,96},{32,0},{64,32},{96,64},{1,97},{33,1},{65,33},{97,65},{2,98}... | collective-permute-start | bytes 393224 | tf_op jit(solution)/shard_map/ppermute | solution.py:32
  87.4 3.1 %collective-permute-done.2.refs_3_ = bf16[8,32,256]{2,1,0:T(8,128)(2,1)S(1)} collective-permute-done((bf16[8,32,256]{2,1,0:T(8,128)(2,1)S(1)}, bf16[8,32,256]{2,1,0:T(8,128)(2,1)S(1)}, u32[]{:S(2)}, u32[]{:S(2)}) %collective-permute-start.2) | collective-permute-done | bytes 131104 | tf_op jit(solution)/shard_map/ppermute | solution.py:32
  90.5 1.9 collective-permute-start.3
  94.3 1.1 more_logits.1
  95.4 6.4 %all-to-all-start.2 = ((f32[16,16,512]{2,1,0:T(8,128)}), f32[16,16,512]{2,1,0:T(8,128)S(1)}, u32[]{:S(2)}, u32[]{:S(2)}) async-start(f32[16,16,512]{2,1,0:T(8,128)} %bitcast.5), calls=%async_computation.2 | async-start | bytes 1048576 | tf_op jit(solution)/shard_map/all_to_all | solution.py:27
  102.1 5.0 %collective-permute-start.4 = (s32[16,5]{1,0:T(8,128)S(1)}, s32[16,5]{1,0:T(8,128)S(1)}, u32[]{:S(2)}, u32[]{:S(2)}) collective-permute-start(s32[16,5]{1,0:T(8,128)S(1)} %copy.32), channel_id=1, source_target_pairs={{0,512},{512,0},{1,513},{513,1},{2,514},{514,2},{3,515},{515,3},{4... | collective-permute-start | bytes 968 | tf_op jit(solution)/shard_map/ppermute | solution.py:32
  107.2 4.3 %collective-permute-done.4 = s32[16,5]{1,0:T(8,128)S(1)} collective-permute-done((s32[16,5]{1,0:T(8,128)S(1)}, s32[16,5]{1,0:T(8,128)S(1)}, u32[]{:S(2)}, u32[]{:S(2)}) %collective-permute-start.4) | collective-permute-done | bytes 352 | tf_op jit(solution)/shard_map/ppermute | solution.py:32
  111.5 2.1 %all-to-all-done.2.part_ref = f32[16,16,512]{2,1,0:T(8,128)S(1)} async-done(((f32[16,16,512]{2,1,0:T(8,128)}), f32[16,16,512]{2,1,0:T(8,128)S(1)}, u32[]{:S(2)}, u32[]{:S(2)}) %all-to-all-start.2) | async-done | bytes 524320 | tf_op jit(solution)/shard_map/all_to_all | solution.py:27
  114.5 13.3 %all_to_all.31 = bf16[16,16,512]{2,1,0:T(8,128)(2,1)S(1)} all-to-all(bf16[16,16,512]{2,1,0:T(8,128)(2,1)S(1)} %get-tuple-element.26), channel_id=1, replica_groups=mesh['za'=2,'zb'=4,'x'=4,'c'=2,'zh'=4,'y'=4] {'x','y'}, dimensions={0} | all-to-all | bytes 524288 | tf_op jit(solution)/shard_map/all_to_all | solution.py:27
  128.2 1.9 collective-permute-start.8
  130.1 1.6 grads.1
  132.0 1.0 add_convert_fusion
  133.0 6.1 %all-to-all-start.4 = ((bf16[16,16,1152]{2,1,0:T(8,128)(2,1)}), bf16[16,16,1152]{2,1,0:T(8,128)(2,1)S(1)}, u32[]{:S(2)}, u32[]{:S(2)}) async-start(bf16[16,16,1152]{2,1,0:T(8,128)(2,1)} %bitcast.12), calls=%async_computation.4 | async-start | bytes 1179648 | tf_op jit(solution)/shard_map/all_to_all | solution.py:27
  139.1 2.3 %collective-permute-start.5 = (bf16[8,32,256]{2,1,0:T(8,128)(2,1)S(1)}, bf16[8,32,256]{2,1,0:T(8,128)(2,1)S(1)}, u32[]{:S(2)}, u32[]{:S(2)}) collective-permute-start(bf16[8,32,256]{2,1,0:T(8,128)(2,1)S(1)} %get-tuple-element.37), channel_id=1, source_target_pairs={{0,32},{32,64},{64,96},{96,0},{1,33},{33,65},{65,97},{97,1},{2,34}... | collective-permute-start | bytes 393224 | tf_op jit(solution)/shard_map/ppermute | solution.py:32
  141.4 4.0 %collective-permute-start.6 = (bf16[8,32,256]{2,1,0:T(8,128)(2,1)S(1)}, bf16[8,32,256]{2,1,0:T(8,128)(2,1)S(1)}, u32[]{:S(2)}, u32[]{:S(2)}) collective-permute-start(bf16[8,32,256]{2,1,0:T(8,128)(2,1)S(1)} %get-tuple-element.36), channel_id=1, source_target_pairs={{0,64},{32,96},{64,0},{96,32},{1,65},{33,97},{65,1},{97,33},{2,66}... | collective-permute-start | bytes 393224 | tf_op jit(solution)/shard_map/ppermute | solution.py:32
  145.4 3.4 %collective-permute-start.7 = (bf16[8,32,256]{2,1,0:T(8,128)(2,1)S(1)}, bf16[8,32,256]{2,1,0:T(8,128)(2,1)S(1)}, u32[]{:S(2)}, u32[]{:S(2)}) collective-permute-start(bf16[8,32,256]{2,1,0:T(8,128)(2,1)S(1)} %get-tuple-element.35), channel_id=1, source_target_pairs={{0,96},{32,0},{64,32},{96,64},{1,97},{33,1},{65,33},{97,65},{2,98}... | collective-permute-start | bytes 393224 | tf_op jit(solution)/shard_map/ppermute | solution.py:32
  148.8 1.2 collective-permute-done.5
  150.0 2.7 %collective-permute-done.7 = bf16[8,32,256]{2,1,0:T(8,128)(2,1)S(1)} collective-permute-done((bf16[8,32,256]{2,1,0:T(8,128)(2,1)S(1)}, bf16[8,32,256]{2,1,0:T(8,128)(2,1)S(1)}, u32[]{:S(2)}, u32[]{:S(2)}) %collective-permute-start.7) | collective-permute-done | bytes 131104 | tf_op jit(solution)/shard_map/ppermute | solution.py:32
  152.7 2.8 %all-to-all-done.4 = bf16[16,16,1152]{2,1,0:T(8,128)(2,1)S(1)} async-done(((bf16[16,16,1152]{2,1,0:T(8,128)(2,1)}), bf16[16,16,1152]{2,1,0:T(8,128)(2,1)S(1)}, u32[]{:S(2)}, u32[]{:S(2)}) %all-to-all-start.4) | async-done | bytes 589856 | tf_op jit(solution)/shard_map/all_to_all | solution.py:27
  156.3 50.2 %all_to_all.32 = bf16[8,72,256]{2,1,0:T(8,128)(2,1)S(1)} all-to-all(bf16[8,72,256]{2,1,0:T(8,128)(2,1)S(1)} %pad_maximum_fusion), channel_id=1, replica_groups=mesh['za'=2,'zb'=4,'x'=4,'c'=2,'zh'=4,'y'=4] {'za','zh'}, dimensions={0} | all-to-all | bytes 589824 | tf_op jit(solution)/shard_map/all_to_all | solution.py:27
  (50 shorter events, 9.6 us)
Async XLA Ops:
  0.6 1.0 copy-start
  1.6 0.8 copy-start.1
  69.7 20.9 %all-to-all-start.1 = ((bf16[16,16,1024]{2,1,0:T(8,128)(2,1)}), bf16[16,16,1024]{2,1,0:T(8,128)(2,1)S(1)}, u32[]{:S(2)}, u32[]{:S(2)}) async-start(bf16[16,16,1024]{2,1,0:T(8,128)(2,1)} %bitcast.3), calls=%async_computation.1 | async-start | bytes 1048576 | tf_op jit(solution)/shard_map/all_to_all | solution.py:27
  75.6 11.4 %collective-permute-start = (bf16[8,32,256]{2,1,0:T(8,128)(2,1)S(1)}, bf16[8,32,256]{2,1,0:T(8,128)(2,1)S(1)}, u32[]{:S(2)}, u32[]{:S(2)}) collective-permute-start(bf16[8,32,256]{2,1,0:T(8,128)(2,1)S(1)} %get-tuple-element.19.refs_0_), channel_id=1, source_target_pairs={{0,32},{32,64},{64,96},{96,0},{1,33},{33,65},{65,97},{97,1},{2,34}... | collective-permute-start | bytes 393224 | tf_op jit(solution)/shard_map/ppermute | solution.py:32
  79.0 8.4 %collective-permute-start.1 = (bf16[8,32,256]{2,1,0:T(8,128)(2,1)S(1)}, bf16[8,32,256]{2,1,0:T(8,128)(2,1)S(1)}, u32[]{:S(2)}, u32[]{:S(2)}) collective-permute-start(bf16[8,32,256]{2,1,0:T(8,128)(2,1)S(1)} %get-tuple-element.19.refs_0_), channel_id=1, source_target_pairs={{0,64},{32,96},{64,0},{96,32},{1,65},{33,97},{65,1},{97,33},{2,66}... | collective-permute-start | bytes 393224 | tf_op jit(solution)/shard_map/ppermute | solution.py:32
  83.7 6.9 %collective-permute-start.2 = (bf16[8,32,256]{2,1,0:T(8,128)(2,1)S(1)}, bf16[8,32,256]{2,1,0:T(8,128)(2,1)S(1)}, u32[]{:S(2)}, u32[]{:S(2)}) collective-permute-start(bf16[8,32,256]{2,1,0:T(8,128)(2,1)S(1)} %get-tuple-element.19.refs_0_), channel_id=1, source_target_pairs={{0,96},{32,0},{64,32},{96,64},{1,97},{33,1},{65,33},{97,65},{2,98}... | collective-permute-start | bytes 393224 | tf_op jit(solution)/shard_map/ppermute | solution.py:32
  90.5 3.8 %collective-permute-start.3 = (bf16[256,1024]{1,0:T(8,128)(2,1)S(1)}, bf16[256,1024]{1,0:T(8,128)(2,1)S(1)}, u32[]{:S(2)}, u32[]{:S(2)}) collective-permute-start(bf16[256,1024]{1,0:T(8,128)(2,1)S(1)} %bitcast.27), channel_id=1, source_target_pairs={{0,16},{16,0},{1,17},{17,1},{2,18},{18,2},{3,19},{19,3},{4,20},{20... | collective-permute-start | bytes 1572872 | tf_op jit(solution)/shard_map/ppermute | solution.py:32
  94.3 7.6 %copy-start.2 = (s32[256,4]{0,1:T(4,128)S(1)}, s32[256,4]{0,1:T(4,128)}, u32[]{:S(2)}) copy-start(s32[256,4]{0,1:T(4,128)} %param.7) | copy-start | bytes 12292
  94.3 7.6 %copy-start.3 = (s32[256]{0:T(256)S(1)}, s32[256]{0:T(256)}, u32[]{:S(2)}) copy-start(s32[256]{0:T(256)} %param.6) | copy-start | bytes 3076
  95.4 18.2 %all-to-all-start.2 = ((f32[16,16,512]{2,1,0:T(8,128)}), f32[16,16,512]{2,1,0:T(8,128)S(1)}, u32[]{:S(2)}, u32[]{:S(2)}) async-start(f32[16,16,512]{2,1,0:T(8,128)} %bitcast.5), calls=%async_computation.2 | async-start | bytes 1048576 | tf_op jit(solution)/shard_map/all_to_all | solution.py:27
  102.1 9.4 %collective-permute-start.4 = (s32[16,5]{1,0:T(8,128)S(1)}, s32[16,5]{1,0:T(8,128)S(1)}, u32[]{:S(2)}, u32[]{:S(2)}) collective-permute-start(s32[16,5]{1,0:T(8,128)S(1)} %copy.32), channel_id=1, source_target_pairs={{0,512},{512,0},{1,513},{513,1},{2,514},{514,2},{3,515},{515,3},{4... | collective-permute-start | bytes 968 | tf_op jit(solution)/shard_map/ppermute | solution.py:32
  128.2 3.8 %collective-permute-start.8 = (bf16[256,1024]{1,0:T(8,128)(2,1)S(1)}, bf16[256,1024]{1,0:T(8,128)(2,1)S(1)}, u32[]{:S(2)}, u32[]{:S(2)}) collective-permute-start(bf16[256,1024]{1,0:T(8,128)(2,1)S(1)} %away.1), channel_id=1, source_target_pairs={{0,16},{16,0},{1,17},{17,1},{2,18},{18,2},{3,19},{19,3},{4,20},{20... | collective-permute-start | bytes 1572872 | tf_op jit(solution)/shard_map/ppermute | solution.py:32
  133.0 22.6 %all-to-all-start.4 = ((bf16[16,16,1152]{2,1,0:T(8,128)(2,1)}), bf16[16,16,1152]{2,1,0:T(8,128)(2,1)S(1)}, u32[]{:S(2)}, u32[]{:S(2)}) async-start(bf16[16,16,1152]{2,1,0:T(8,128)(2,1)} %bitcast.12), calls=%async_computation.4 | async-start | bytes 1179648 | tf_op jit(solution)/shard_map/all_to_all | solution.py:27
  139.1 11.0 %collective-permute-start.5 = (bf16[8,32,256]{2,1,0:T(8,128)(2,1)S(1)}, bf16[8,32,256]{2,1,0:T(8,128)(2,1)S(1)}, u32[]{:S(2)}, u32[]{:S(2)}) collective-permute-start(bf16[8,32,256]{2,1,0:T(8,128)(2,1)S(1)} %get-tuple-element.37), channel_id=1, source_target_pairs={{0,32},{32,64},{64,96},{96,0},{1,33},{33,65},{65,97},{97,1},{2,34}... | collective-permute-start | bytes 393224 | tf_op jit(solution)/shard_map/ppermute | solution.py:32
  141.4 8.7 %collective-permute-start.6 = (bf16[8,32,256]{2,1,0:T(8,128)(2,1)S(1)}, bf16[8,32,256]{2,1,0:T(8,128)(2,1)S(1)}, u32[]{:S(2)}, u32[]{:S(2)}) collective-permute-start(bf16[8,32,256]{2,1,0:T(8,128)(2,1)S(1)} %get-tuple-element.36), channel_id=1, source_target_pairs={{0,64},{32,96},{64,0},{96,32},{1,65},{33,97},{65,1},{97,33},{2,66}... | collective-permute-start | bytes 393224 | tf_op jit(solution)/shard_map/ppermute | solution.py:32
  145.4 7.4 %collective-permute-start.7 = (bf16[8,32,256]{2,1,0:T(8,128)(2,1)S(1)}, bf16[8,32,256]{2,1,0:T(8,128)(2,1)S(1)}, u32[]{:S(2)}, u32[]{:S(2)}) collective-permute-start(bf16[8,32,256]{2,1,0:T(8,128)(2,1)S(1)} %get-tuple-element.35), channel_id=1, source_target_pairs={{0,96},{32,0},{64,32},{96,64},{1,97},{33,1},{65,33},{97,65},{2,98}... | collective-permute-start | bytes 393224 | tf_op jit(solution)/shard_map/ppermute | solution.py:32

commit v6 on v5

--- a/solution.py
+++ b/solution.py
@@ -32,7 +32,15 @@
     return lax.ppermute(x, axis, [(i, (i + by) % n) for i in range(n)])
 
 
-def pack_kernel(q_ref, p_ref, out_ref, rows_ref):
+def pack_kernel(q_in, p_in, out_ref, q_ref, p_ref, rows_ref, sems):
+    copies = [
+        pltpu.make_async_copy(p_in, p_ref, sems.at[0]),
+        pltpu.make_async_copy(q_in, q_ref, sems.at[1]),
+    ]
+    for copy in copies:
+        copy.start()
+    for copy in copies:
+        copy.wait()
     groups, _, k = out_ref.shape
     n = q_ref.shape[0] // groups
     own, d = p_ref.shape
@@ -162,12 +170,18 @@
     prow = own * d // k
     send = pl.pallas_call(
         pack_kernel,
+        in_specs=[pl.BlockSpec(memory_space=pl.ANY)] * 2,
         out_shape=jax.ShapeDtypeStruct((A, n + prow, k), bf16),
-        scratch_shapes=[pltpu.VMEM((prow, k), f32)],
-        compiler_params=params,
+        scratch_shapes=[
+            pltpu.VMEM((nq, k), f32),
+            pltpu.VMEM((own, d), f32),
+            pltpu.VMEM((prow, k), f32),
+            pltpu.SemaphoreType.DMA((2,)),
+        ],
+        compiler_params=pltpu.CompilerParams(vmem_limit_bytes=60 * 2**20),
         name="pack",
     )(queries, passages)
-    got = exchange(send, FAR)
+    got, other = lax.optimization_barrier((exchange(send, FAR), other))
     ids = jnp.where(y // 2 == za, mine, other)
     q = got[:, :n]
     qs = [q] + [shift(q, "x", j) for j in range(1, X)]

time: 210 us -> 209 us (level)
  blocking collectives: 130 us -> 62.2 us
  waiting for transfers between devices: 17.9 us -> 53.6 us
  starting transfers between devices: 48.4 us -> 78.6 us
    all_to_all x3 -> x2, blocking collectives: 130 us -> 62.2 us  [exchange(): return lax.all_to_all(x, axes, 0, 0, tiled=True)]
    all_to_all x3 -> x4, starting transfers between devices: 18.4 us -> 45.9 us  [exchange(): return lax.all_to_all(x, axes, 0, 0, tiled=True)]
    all_to_all x3 -> x4, waiting for transfers between devices: 4.97 us -> 30.4 us  [exchange(): return lax.all_to_all(x, axes, 0, 0, tiled=True)]
    ppermute x9, waiting for transfers between devices: 13 us -> 23.2 us  [shift(): return lax.ppermute(x, axis, [(i, (i + by) % n) for i in range(n)])]
    ppermute x9, starting transfers between devices: 29.9 us -> 32.7 us  [shift(): return lax.ppermute(x, axis, [(i, (i + by) % n) for i in range(n)])]
  transfers between devices with their start and end apart: 12 -> 13, of which waited for: 9 -> 10; matrix products, arithmetic and copies ran while one was open for 0% -> 1% of each run, Pallas kernels for 1% -> 1%
where the time goes in v6:
time: 209 us; the launch traced here: 208 us
  starting transfers between devices  78.6 us (38%)
  blocking collectives  62.2 us (30%)
  waiting for transfers between devices  53.6 us (26%)
  Pallas kernels  6.48 us (3%)
  local copies, waits for them, and re-layouts  3.09 us (1%)
  other arithmetic  2.77 us (1%)
    all_to_all x2, blocking collectives, exchange(): return lax.all_to_all(x, axes, 0, 0, tiled=True)  62.2 us
    all_to_all x4, starting transfers between devices, exchange(): return lax.all_to_all(x, axes, 0, 0, tiled=True)  45.9 us
    ppermute x9, starting transfers between devices, shift(): return lax.ppermute(x, axis, [(i, (i + by) % n) for i in range(n)])  32.7 us
    all_to_all x4, waiting for transfers between devices, exchange(): return lax.all_to_all(x, axes, 0, 0, tiled=True)  30.4 us
    ppermute x9, waiting for transfers between devices, shift(): return lax.ppermute(x, axis, [(i, (i + by) % n) for i in range(n)])  23.2 us
  transfers between devices with their start and end apart: 13, of which 10 were waited for; matrix products, arithmetic and copies ran while one was open for 1% of the time, Pallas kernels for 1%

profile of v6, /device:TPU:32, one launch (start us, length us, event | category | flops | bytes accessed | tf_op | source)
XLA Modules:
  0.0 207.6 jit_solution(12283068823849711656)
XLA Ops:
  0.6 1.7 pack.1
  2.4 27.5 %all-to-all-start = ((bf16[8,64,256]{2,1,0:T(8,128)(2,1)}), bf16[8,64,256]{2,1,0:T(8,128)(2,1)S(1)}, u32[]{:S(2)}, u32[]{:S(2)}) async-start(bf16[8,64,256]{2,1,0:T(8,128)(2,1)} %pack.1), calls=%async_computation | async-start | bytes 524288 | tf_op jit(solution)/shard_map/all_to_all | solution.py:27
  30.7 7.8 %collective-permute-start = (s32[16,5]{1,0:T(8,128)S(1)}, s32[16,5]{1,0:T(8,128)S(1)}, u32[]{:S(2)}, u32[]{:S(2)}) collective-permute-start(s32[16,5]{1,0:T(8,128)S(1)} %copy.31), channel_id=1, source_target_pairs={{0,512},{512,0},{1,513},{513,1},{2,514},{514,2},{3,515},{515,3},{4... | collective-permute-start | bytes 968 | tf_op jit(solution)/shard_map/ppermute | solution.py:32
  38.5 14.5 %collective-permute-done = s32[16,5]{1,0:T(8,128)S(1)} collective-permute-done((s32[16,5]{1,0:T(8,128)S(1)}, s32[16,5]{1,0:T(8,128)S(1)}, u32[]{:S(2)}, u32[]{:S(2)}) %collective-permute-start) | collective-permute-done | bytes 352 | tf_op jit(solution)/shard_map/ppermute | solution.py:32
  53.0 15.9 %all-to-all-done = bf16[8,64,256]{2,1,0:T(8,128)(2,1)S(1)} async-done(((bf16[8,64,256]{2,1,0:T(8,128)(2,1)}), bf16[8,64,256]{2,1,0:T(8,128)(2,1)S(1)}, u32[]{:S(2)}, u32[]{:S(2)}) %all-to-all-start) | async-done | bytes 262176 | tf_op jit(solution)/shard_map/all_to_all | solution.py:27
  70.0 5.9 %all-to-all-start.1 = ((bf16[16,16,1024]{2,1,0:T(8,128)(2,1)}), bf16[16,16,1024]{2,1,0:T(8,128)(2,1)S(1)}, u32[]{:S(2)}, u32[]{:S(2)}) async-start(bf16[16,16,1024]{2,1,0:T(8,128)(2,1)} %bitcast.4), calls=%async_computation.1 | async-start | bytes 1048576 | tf_op jit(solution)/shard_map/all_to_all | solution.py:27
  76.0 3.4 %collective-permute-start.1 = (bf16[8,32,256]{2,1,0:T(8,128)(2,1)S(1)}, bf16[8,32,256]{2,1,0:T(8,128)(2,1)S(1)}, u32[]{:S(2)}, u32[]{:S(2)}) collective-permute-start(bf16[8,32,256]{2,1,0:T(8,128)(2,1)S(1)} %get-tuple-element.22.refs_0_), channel_id=1, source_target_pairs={{0,32},{32,64},{64,96},{96,0},{1,33},{33,65},{65,97},{97,1},{2,34}... | collective-permute-start | bytes 393224 | tf_op jit(solution)/shard_map/ppermute | solution.py:32
  79.4 4.6 %collective-permute-start.2 = (bf16[8,32,256]{2,1,0:T(8,128)(2,1)S(1)}, bf16[8,32,256]{2,1,0:T(8,128)(2,1)S(1)}, u32[]{:S(2)}, u32[]{:S(2)}) collective-permute-start(bf16[8,32,256]{2,1,0:T(8,128)(2,1)S(1)} %get-tuple-element.22.refs_0_), channel_id=1, source_target_pairs={{0,64},{32,96},{64,0},{96,32},{1,65},{33,97},{65,1},{97,33},{2,66}... | collective-permute-start | bytes 393224 | tf_op jit(solution)/shard_map/ppermute | solution.py:32
  84.0 3.3 %collective-permute-start.3 = (bf16[8,32,256]{2,1,0:T(8,128)(2,1)S(1)}, bf16[8,32,256]{2,1,0:T(8,128)(2,1)S(1)}, u32[]{:S(2)}, u32[]{:S(2)}) collective-permute-start(bf16[8,32,256]{2,1,0:T(8,128)(2,1)S(1)} %get-tuple-element.22.refs_0_), channel_id=1, source_target_pairs={{0,96},{32,0},{64,32},{96,64},{1,97},{33,1},{65,33},{97,65},{2,98}... | collective-permute-start | bytes 393224 | tf_op jit(solution)/shard_map/ppermute | solution.py:32
  87.7 3.1 %collective-permute-done.3.refs_3_ = bf16[8,32,256]{2,1,0:T(8,128)(2,1)S(1)} collective-permute-done((bf16[8,32,256]{2,1,0:T(8,128)(2,1)S(1)}, bf16[8,32,256]{2,1,0:T(8,128)(2,1)S(1)}, u32[]{:S(2)}, u32[]{:S(2)}) %collective-permute-start.3) | collective-permute-done | bytes 131104 | tf_op jit(solution)/shard_map/ppermute | solution.py:32
  90.9 1.9 collective-permute-start.4
  95.8 6.4 %all-to-all-start.2 = ((f32[16,16,512]{2,1,0:T(8,128)}), f32[16,16,512]{2,1,0:T(8,128)S(1)}, u32[]{:S(2)}, u32[]{:S(2)}) async-start(f32[16,16,512]{2,1,0:T(8,128)} %bitcast.6), calls=%async_computation.2 | async-start | bytes 1048576 | tf_op jit(solution)/shard_map/all_to_all | solution.py:27
  102.3 11.7 %all-to-all-done.2.part_ref = f32[16,16,512]{2,1,0:T(8,128)S(1)} async-done(((f32[16,16,512]{2,1,0:T(8,128)}), f32[16,16,512]{2,1,0:T(8,128)S(1)}, u32[]{:S(2)}, u32[]{:S(2)}) %all-to-all-start.2) | async-done | bytes 524320 | tf_op jit(solution)/shard_map/all_to_all | solution.py:27
  114.9 11.7 %all_to_all.30 = bf16[16,16,512]{2,1,0:T(8,128)(2,1)S(1)} all-to-all(bf16[16,16,512]{2,1,0:T(8,128)(2,1)S(1)} %get-tuple-element.30), channel_id=1, replica_groups=mesh['za'=2,'zb'=4,'x'=4,'c'=2,'zh'=4,'y'=4] {'x','y'}, dimensions={0} | all-to-all | bytes 524288 | tf_op jit(solution)/shard_map/all_to_all | solution.py:27
  126.9 1.9 collective-permute-start.8
  128.9 1.6 grads.1
  131.7 6.1 %all-to-all-start.4 = ((bf16[16,16,1152]{2,1,0:T(8,128)(2,1)}), bf16[16,16,1152]{2,1,0:T(8,128)(2,1)S(1)}, u32[]{:S(2)}, u32[]{:S(2)}) async-start(bf16[16,16,1152]{2,1,0:T(8,128)(2,1)} %bitcast.12), calls=%async_computation.4 | async-start | bytes 1179648 | tf_op jit(solution)/shard_map/all_to_all | solution.py:27
  137.8 2.3 %collective-permute-start.5 = (bf16[8,32,256]{2,1,0:T(8,128)(2,1)S(1)}, bf16[8,32,256]{2,1,0:T(8,128)(2,1)S(1)}, u32[]{:S(2)}, u32[]{:S(2)}) collective-permute-start(bf16[8,32,256]{2,1,0:T(8,128)(2,1)S(1)} %get-tuple-element.41), channel_id=1, source_target_pairs={{0,32},{32,64},{64,96},{96,0},{1,33},{33,65},{65,97},{97,1},{2,34}... | collective-permute-start | bytes 393224 | tf_op jit(solution)/shard_map/ppermute | solution.py:32
  140.1 4.0 %collective-permute-start.6 = (bf16[8,32,256]{2,1,0:T(8,128)(2,1)S(1)}, bf16[8,32,256]{2,1,0:T(8,128)(2,1)S(1)}, u32[]{:S(2)}, u32[]{:S(2)}) collective-permute-start(bf16[8,32,256]{2,1,0:T(8,128)(2,1)S(1)} %get-tuple-element.40), channel_id=1, source_target_pairs={{0,64},{32,96},{64,0},{96,32},{1,65},{33,97},{65,1},{97,33},{2,66}... | collective-permute-start | bytes 393224 | tf_op jit(solution)/shard_map/ppermute | solution.py:32
  144.1 3.4 %collective-permute-start.7 = (bf16[8,32,256]{2,1,0:T(8,128)(2,1)S(1)}, bf16[8,32,256]{2,1,0:T(8,128)(2,1)S(1)}, u32[]{:S(2)}, u32[]{:S(2)}) collective-permute-start(bf16[8,32,256]{2,1,0:T(8,128)(2,1)S(1)} %get-tuple-element.39), channel_id=1, source_target_pairs={{0,96},{32,0},{64,32},{96,64},{1,97},{33,1},{65,33},{97,65},{2,98}... | collective-permute-start | bytes 393224 | tf_op jit(solution)/shard_map/ppermute | solution.py:32
  147.5 1.2 collective-permute-done.5
  148.7 2.7 %collective-permute-done.7 = bf16[8,32,256]{2,1,0:T(8,128)(2,1)S(1)} collective-permute-done((bf16[8,32,256]{2,1,0:T(8,128)(2,1)S(1)}, bf16[8,32,256]{2,1,0:T(8,128)(2,1)S(1)}, u32[]{:S(2)}, u32[]{:S(2)}) %collective-permute-start.7) | collective-permute-done | bytes 131104 | tf_op jit(solution)/shard_map/ppermute | solution.py:32
  151.4 2.8 %all-to-all-done.4 = bf16[16,16,1152]{2,1,0:T(8,128)(2,1)S(1)} async-done(((bf16[16,16,1152]{2,1,0:T(8,128)(2,1)}), bf16[16,16,1152]{2,1,0:T(8,128)(2,1)S(1)}, u32[]{:S(2)}, u32[]{:S(2)}) %all-to-all-start.4) | async-done | bytes 589856 | tf_op jit(solution)/shard_map/all_to_all | solution.py:27
  155.0 50.5 %all_to_all.31 = bf16[8,72,256]{2,1,0:T(8,128)(2,1)S(1)} all-to-all(bf16[8,72,256]{2,1,0:T(8,128)(2,1)S(1)} %pad_maximum_fusion), channel_id=1, replica_groups=mesh['za'=2,'zb'=4,'x'=4,'c'=2,'zh'=4,'y'=4] {'za','zh'}, dimensions={0} | all-to-all | bytes 589824 | tf_op jit(solution)/shard_map/all_to_all | solution.py:27
  (43 shorter events, 10.6 us)
Async XLA Ops:
  2.4 66.6 %all-to-all-start = ((bf16[8,64,256]{2,1,0:T(8,128)(2,1)}), bf16[8,64,256]{2,1,0:T(8,128)(2,1)S(1)}, u32[]{:S(2)}, u32[]{:S(2)}) async-start(bf16[8,64,256]{2,1,0:T(8,128)(2,1)} %pack.1), calls=%async_computation | async-start | bytes 524288 | tf_op jit(solution)/shard_map/all_to_all | solution.py:27
  30.7 22.4 %collective-permute-start = (s32[16,5]{1,0:T(8,128)S(1)}, s32[16,5]{1,0:T(8,128)S(1)}, u32[]{:S(2)}, u32[]{:S(2)}) collective-permute-start(s32[16,5]{1,0:T(8,128)S(1)} %copy.31), channel_id=1, source_target_pairs={{0,512},{512,0},{1,513},{513,1},{2,514},{514,2},{3,515},{515,3},{4... | collective-permute-start | bytes 968 | tf_op jit(solution)/shard_map/ppermute | solution.py:32
  70.0 20.9 %all-to-all-start.1 = ((bf16[16,16,1024]{2,1,0:T(8,128)(2,1)}), bf16[16,16,1024]{2,1,0:T(8,128)(2,1)S(1)}, u32[]{:S(2)}, u32[]{:S(2)}) async-start(bf16[16,16,1024]{2,1,0:T(8,128)(2,1)} %bitcast.4), calls=%async_computation.1 | async-start | bytes 1048576 | tf_op jit(solution)/shard_map/all_to_all | solution.py:27
  76.0 11.4 %collective-permute-start.1 = (bf16[8,32,256]{2,1,0:T(8,128)(2,1)S(1)}, bf16[8,32,256]{2,1,0:T(8,128)(2,1)S(1)}, u32[]{:S(2)}, u32[]{:S(2)}) collective-permute-start(bf16[8,32,256]{2,1,0:T(8,128)(2,1)S(1)} %get-tuple-element.22.refs_0_), channel_id=1, source_target_pairs={{0,32},{32,64},{64,96},{96,0},{1,33},{33,65},{65,97},{97,1},{2,34}... | collective-permute-start | bytes 393224 | tf_op jit(solution)/shard_map/ppermute | solution.py:32
  79.4 8.4 %collective-permute-start.2 = (bf16[8,32,256]{2,1,0:T(8,128)(2,1)S(1)}, bf16[8,32,256]{2,1,0:T(8,128)(2,1)S(1)}, u32[]{:S(2)}, u32[]{:S(2)}) collective-permute-start(bf16[8,32,256]{2,1,0:T(8,128)(2,1)S(1)} %get-tuple-element.22.refs_0_), channel_id=1, source_target_pairs={{0,64},{32,96},{64,0},{96,32},{1,65},{33,97},{65,1},{97,33},{2,66}... | collective-permute-start | bytes 393224 | tf_op jit(solution)/shard_map/ppermute | solution.py:32
  84.0 6.9 %collective-permute-start.3 = (bf16[8,32,256]{2,1,0:T(8,128)(2,1)S(1)}, bf16[8,32,256]{2,1,0:T(8,128)(2,1)S(1)}, u32[]{:S(2)}, u32[]{:S(2)}) collective-permute-start(bf16[8,32,256]{2,1,0:T(8,128)(2,1)S(1)} %get-tuple-element.22.refs_0_), channel_id=1, source_target_pairs={{0,96},{32,0},{64,32},{96,64},{1,97},{33,1},{65,33},{97,65},{2,98}... | collective-permute-start | bytes 393224 | tf_op jit(solution)/shard_map/ppermute | solution.py:32
  90.9 3.8 %collective-permute-start.4 = (bf16[256,1024]{1,0:T(8,128)(2,1)S(1)}, bf16[256,1024]{1,0:T(8,128)(2,1)S(1)}, u32[]{:S(2)}, u32[]{:S(2)}) collective-permute-start(bf16[256,1024]{1,0:T(8,128)(2,1)S(1)} %bitcast.27), channel_id=1, source_target_pairs={{0,16},{16,0},{1,17},{17,1},{2,18},{18,2},{3,19},{19,3},{4,20},{20... | collective-permute-start | bytes 1572872 | tf_op jit(solution)/shard_map/ppermute | solution.py:32
  95.8 18.2 %all-to-all-start.2 = ((f32[16,16,512]{2,1,0:T(8,128)}), f32[16,16,512]{2,1,0:T(8,128)S(1)}, u32[]{:S(2)}, u32[]{:S(2)}) async-start(f32[16,16,512]{2,1,0:T(8,128)} %bitcast.6), calls=%async_computation.2 | async-start | bytes 1048576 | tf_op jit(solution)/shard_map/all_to_all | solution.py:27
  126.9 3.8 %collective-permute-start.8 = (bf16[256,1024]{1,0:T(8,128)(2,1)S(1)}, bf16[256,1024]{1,0:T(8,128)(2,1)S(1)}, u32[]{:S(2)}, u32[]{:S(2)}) collective-permute-start(bf16[256,1024]{1,0:T(8,128)(2,1)S(1)} %away.1), channel_id=1, source_target_pairs={{0,16},{16,0},{1,17},{17,1},{2,18},{18,2},{3,19},{19,3},{4,20},{20... | collective-permute-start | bytes 1572872 | tf_op jit(solution)/shard_map/ppermute | solution.py:32
  131.7 22.6 %all-to-all-start.4 = ((bf16[16,16,1152]{2,1,0:T(8,128)(2,1)}), bf16[16,16,1152]{2,1,0:T(8,128)(2,1)S(1)}, u32[]{:S(2)}, u32[]{:S(2)}) async-start(bf16[16,16,1152]{2,1,0:T(8,128)(2,1)} %bitcast.12), calls=%async_computation.4 | async-start | bytes 1179648 | tf_op jit(solution)/shard_map/all_to_all | solution.py:27
  137.8 11.0 %collective-permute-start.5 = (bf16[8,32,256]{2,1,0:T(8,128)(2,1)S(1)}, bf16[8,32,256]{2,1,0:T(8,128)(2,1)S(1)}, u32[]{:S(2)}, u32[]{:S(2)}) collective-permute-start(bf16[8,32,256]{2,1,0:T(8,128)(2,1)S(1)} %get-tuple-element.41), channel_id=1, source_target_pairs={{0,32},{32,64},{64,96},{96,0},{1,33},{33,65},{65,97},{97,1},{2,34}... | collective-permute-start | bytes 393224 | tf_op jit(solution)/shard_map/ppermute | solution.py:32
  140.1 8.6 %collective-permute-start.6 = (bf16[8,32,256]{2,1,0:T(8,128)(2,1)S(1)}, bf16[8,32,256]{2,1,0:T(8,128)(2,1)S(1)}, u32[]{:S(2)}, u32[]{:S(2)}) collective-permute-start(bf16[8,32,256]{2,1,0:T(8,128)(2,1)S(1)} %get-tuple-element.40), channel_id=1, source_target_pairs={{0,64},{32,96},{64,0},{96,32},{1,65},{33,97},{65,1},{97,33},{2,66}... | collective-permute-start | bytes 393224 | tf_op jit(solution)/shard_map/ppermute | solution.py:32
  144.1 7.4 %collective-permute-start.7 = (bf16[8,32,256]{2,1,0:T(8,128)(2,1)S(1)}, bf16[8,32,256]{2,1,0:T(8,128)(2,1)S(1)}, u32[]{:S(2)}, u32[]{:S(2)}) collective-permute-start(bf16[8,32,256]{2,1,0:T(8,128)(2,1)S(1)} %get-tuple-element.39), channel_id=1, source_target_pairs={{0,96},{32,0},{64,32},{96,64},{1,97},{33,1},{65,33},{97,65},{2,98}... | collective-permute-start | bytes 393224 | tf_op jit(solution)/shard_map/ppermute | solution.py:32

commit v7 on v6

--- a/solution.py
+++ b/solution.py
@@ -152,6 +152,20 @@
                 qg_ref[j, za * ZH + s] = terms[za * n : (za + 1) * n, s * k : (s + 1) * k]
 
 
+def finish_kernel(got_ref, qg_ref, pg_ref):
+    groups, _, k = got_ref.shape
+    n = qg_ref.shape[0] // groups
+    own, d = pg_ref.shape
+    prow = own * d // k
+    total = jnp.zeros((prow, k), f32)
+    for g in range(groups):
+        qg_ref[g * n : (g + 1) * n, :] = got_ref[g, :n].astype(f32)
+        total = total + got_ref[g, n : n + prow].astype(f32)
+    for i in range(prow):
+        r, t = divmod(i, d // k)
+        pg_ref[r : r + 1, t * k : (t + 1) * k] = total[i : i + 1, :]
+
+
 def on_device(queries, passages, positive, hard_negs):
     nq, k = queries.shape
     own, d = passages.shape
@@ -259,8 +273,15 @@
     loss = jnp.pad(loss, ((0, 0), (0, 7), (0, k - 3 * n)))
     loss = jnp.broadcast_to(loss[:, None], (ZA, ZH, 8, k)).reshape(A, 8, k)
     got = exchange(jnp.concatenate([qg, pg, loss], axis=1), FAR)
-    qg = got[:, :n].reshape(nq, k).astype(f32)
-    pg = jnp.sum(got[:, n : n + prow].astype(f32), axis=0).reshape(own, d)
+    qg, pg = pl.pallas_call(
+        finish_kernel,
+        out_shape=(
+            jax.ShapeDtypeStruct((nq, k), f32),
+            jax.ShapeDtypeStruct((own, d), f32),
+        ),
+        compiler_params=params,
+        name="finish",
+    )(got)
     loss = got[:, n + prow, : 3 * n].astype(f32).reshape(A, 3, n)
     row_loss = (loss[:, 0] + loss[:, 1] + loss[:, 2]).reshape(nq)
     return row_loss, qg, pg

time: 209 us -> 208 us (level)
  no operation moved by 1% of the time
where the time goes in v7:
time: 208 us; the launch traced here: 207 us
  starting transfers between devices  78.6 us (38%)
  blocking collectives  62.2 us (30%)
  waiting for transfers between devices  53.6 us (26%)
  Pallas kernels  7.21 us (3%)
  local copies, waits for them, and re-layouts  2.44 us (1%)
    all_to_all x2, blocking collectives, exchange(): return lax.all_to_all(x, axes, 0, 0, tiled=True)  62.2 us
    all_to_all x4, starting transfers between devices, exchange(): return lax.all_to_all(x, axes, 0, 0, tiled=True)  45.9 us
    ppermute x9, starting transfers between devices, shift(): return lax.ppermute(x, axis, [(i, (i + by) % n) for i in range(n)])  32.7 us
    all_to_all x4, waiting for transfers between devices, exchange(): return lax.all_to_all(x, axes, 0, 0, tiled=True)  30.4 us
    ppermute x9, waiting for transfers between devices, shift(): return lax.ppermute(x, axis, [(i, (i + by) % n) for i in range(n)])  23.2 us
  transfers between devices with their start and end apart: 13, of which 10 were waited for; matrix products, arithmetic and copies ran while one was open for 1% of the time, Pallas kernels for 1%

profile of v7, /device:TPU:32, one launch (start us, length us, event | category | flops | bytes accessed | tf_op | source)
XLA Modules:
  0.0 207.0 jit_solution(4443556635414177496)
XLA Ops:
  0.6 1.7 pack.1
  2.4 27.5 %all-to-all-start = ((bf16[8,64,256]{2,1,0:T(8,128)(2,1)}), bf16[8,64,256]{2,1,0:T(8,128)(2,1)S(1)}, u32[]{:S(2)}, u32[]{:S(2)}) async-start(bf16[8,64,256]{2,1,0:T(8,128)(2,1)} %pack.1), calls=%async_computation | async-start | bytes 524288 | tf_op jit(solution)/shard_map/all_to_all | solution.py:27
  30.7 7.8 %collective-permute-start = (s32[16,5]{1,0:T(8,128)S(1)}, s32[16,5]{1,0:T(8,128)S(1)}, u32[]{:S(2)}, u32[]{:S(2)}) collective-permute-start(s32[16,5]{1,0:T(8,128)S(1)} %copy.32), channel_id=1, source_target_pairs={{0,512},{512,0},{1,513},{513,1},{2,514},{514,2},{3,515},{515,3},{4... | collective-permute-start | bytes 968 | tf_op jit(solution)/shard_map/ppermute | solution.py:32
  38.5 14.5 %collective-permute-done = s32[16,5]{1,0:T(8,128)S(1)} collective-permute-done((s32[16,5]{1,0:T(8,128)S(1)}, s32[16,5]{1,0:T(8,128)S(1)}, u32[]{:S(2)}, u32[]{:S(2)}) %collective-permute-start) | collective-permute-done | bytes 352 | tf_op jit(solution)/shard_map/ppermute | solution.py:32
  53.0 15.9 %all-to-all-done = bf16[8,64,256]{2,1,0:T(8,128)(2,1)S(1)} async-done(((bf16[8,64,256]{2,1,0:T(8,128)(2,1)}), bf16[8,64,256]{2,1,0:T(8,128)(2,1)S(1)}, u32[]{:S(2)}, u32[]{:S(2)}) %all-to-all-start) | async-done | bytes 262176 | tf_op jit(solution)/shard_map/all_to_all | solution.py:27
  70.0 5.9 %all-to-all-start.1 = ((bf16[16,16,1024]{2,1,0:T(8,128)(2,1)}), bf16[16,16,1024]{2,1,0:T(8,128)(2,1)S(1)}, u32[]{:S(2)}, u32[]{:S(2)}) async-start(bf16[16,16,1024]{2,1,0:T(8,128)(2,1)} %bitcast.4), calls=%async_computation.1 | async-start | bytes 1048576 | tf_op jit(solution)/shard_map/all_to_all | solution.py:27
  76.0 3.4 %collective-permute-start.1 = (bf16[8,32,256]{2,1,0:T(8,128)(2,1)S(1)}, bf16[8,32,256]{2,1,0:T(8,128)(2,1)S(1)}, u32[]{:S(2)}, u32[]{:S(2)}) collective-permute-start(bf16[8,32,256]{2,1,0:T(8,128)(2,1)S(1)} %get-tuple-element.24.refs_0_), channel_id=1, source_target_pairs={{0,32},{32,64},{64,96},{96,0},{1,33},{33,65},{65,97},{97,1},{2,34}... | collective-permute-start | bytes 393224 | tf_op jit(solution)/shard_map/ppermute | solution.py:32
  79.4 4.6 %collective-permute-start.2 = (bf16[8,32,256]{2,1,0:T(8,128)(2,1)S(1)}, bf16[8,32,256]{2,1,0:T(8,128)(2,1)S(1)}, u32[]{:S(2)}, u32[]{:S(2)}) collective-permute-start(bf16[8,32,256]{2,1,0:T(8,128)(2,1)S(1)} %get-tuple-element.24.refs_0_), channel_id=1, source_target_pairs={{0,64},{32,96},{64,0},{96,32},{1,65},{33,97},{65,1},{97,33},{2,66}... | collective-permute-start | bytes 393224 | tf_op jit(solution)/shard_map/ppermute | solution.py:32
  84.0 3.3 %collective-permute-start.3 = (bf16[8,32,256]{2,1,0:T(8,128)(2,1)S(1)}, bf16[8,32,256]{2,1,0:T(8,128)(2,1)S(1)}, u32[]{:S(2)}, u32[]{:S(2)}) collective-permute-start(bf16[8,32,256]{2,1,0:T(8,128)(2,1)S(1)} %get-tuple-element.24.refs_0_), channel_id=1, source_target_pairs={{0,96},{32,0},{64,32},{96,64},{1,97},{33,1},{65,33},{97,65},{2,98}... | collective-permute-start | bytes 393224 | tf_op jit(solution)/shard_map/ppermute | solution.py:32
  87.7 3.1 %collective-permute-done.3.refs_3_ = bf16[8,32,256]{2,1,0:T(8,128)(2,1)S(1)} collective-permute-done((bf16[8,32,256]{2,1,0:T(8,128)(2,1)S(1)}, bf16[8,32,256]{2,1,0:T(8,128)(2,1)S(1)}, u32[]{:S(2)}, u32[]{:S(2)}) %collective-permute-start.3) | collective-permute-done | bytes 131104 | tf_op jit(solution)/shard_map/ppermute | solution.py:32
  90.9 1.9 collective-permute-start.4
  95.8 6.4 %all-to-all-start.2 = ((f32[16,16,512]{2,1,0:T(8,128)}), f32[16,16,512]{2,1,0:T(8,128)S(1)}, u32[]{:S(2)}, u32[]{:S(2)}) async-start(f32[16,16,512]{2,1,0:T(8,128)} %bitcast.6), calls=%async_computation.2 | async-start | bytes 1048576 | tf_op jit(solution)/shard_map/all_to_all | solution.py:27
  102.3 11.7 %all-to-all-done.2.part_ref = f32[16,16,512]{2,1,0:T(8,128)S(1)} async-done(((f32[16,16,512]{2,1,0:T(8,128)}), f32[16,16,512]{2,1,0:T(8,128)S(1)}, u32[]{:S(2)}, u32[]{:S(2)}) %all-to-all-start.2) | async-done | bytes 524320 | tf_op jit(solution)/shard_map/all_to_all | solution.py:27
  114.9 11.7 %all_to_all.30 = bf16[16,16,512]{2,1,0:T(8,128)(2,1)S(1)} all-to-all(bf16[16,16,512]{2,1,0:T(8,128)(2,1)S(1)} %get-tuple-element.32), channel_id=1, replica_groups=mesh['za'=2,'zb'=4,'x'=4,'c'=2,'zh'=4,'y'=4] {'x','y'}, dimensions={0} | all-to-all | bytes 524288 | tf_op jit(solution)/shard_map/all_to_all | solution.py:27
  126.9 1.9 collective-permute-start.8
  128.9 1.6 grads.1
  131.7 6.1 %all-to-all-start.4 = ((bf16[16,16,1152]{2,1,0:T(8,128)(2,1)}), bf16[16,16,1152]{2,1,0:T(8,128)(2,1)S(1)}, u32[]{:S(2)}, u32[]{:S(2)}) async-start(bf16[16,16,1152]{2,1,0:T(8,128)(2,1)} %bitcast.12), calls=%async_computation.4 | async-start | bytes 1179648 | tf_op jit(solution)/shard_map/all_to_all | solution.py:27
  137.8 2.3 %collective-permute-start.5 = (bf16[8,32,256]{2,1,0:T(8,128)(2,1)S(1)}, bf16[8,32,256]{2,1,0:T(8,128)(2,1)S(1)}, u32[]{:S(2)}, u32[]{:S(2)}) collective-permute-start(bf16[8,32,256]{2,1,0:T(8,128)(2,1)S(1)} %get-tuple-element.45), channel_id=1, source_target_pairs={{0,32},{32,64},{64,96},{96,0},{1,33},{33,65},{65,97},{97,1},{2,34}... | collective-permute-start | bytes 393224 | tf_op jit(solution)/shard_map/ppermute | solution.py:32
  140.1 4.0 %collective-permute-start.6 = (bf16[8,32,256]{2,1,0:T(8,128)(2,1)S(1)}, bf16[8,32,256]{2,1,0:T(8,128)(2,1)S(1)}, u32[]{:S(2)}, u32[]{:S(2)}) collective-permute-start(bf16[8,32,256]{2,1,0:T(8,128)(2,1)S(1)} %get-tuple-element.44), channel_id=1, source_target_pairs={{0,64},{32,96},{64,0},{96,32},{1,65},{33,97},{65,1},{97,33},{2,66}... | collective-permute-start | bytes 393224 | tf_op jit(solution)/shard_map/ppermute | solution.py:32
  144.1 3.4 %collective-permute-start.7 = (bf16[8,32,256]{2,1,0:T(8,128)(2,1)S(1)}, bf16[8,32,256]{2,1,0:T(8,128)(2,1)S(1)}, u32[]{:S(2)}, u32[]{:S(2)}) collective-permute-start(bf16[8,32,256]{2,1,0:T(8,128)(2,1)S(1)} %get-tuple-element.43), channel_id=1, source_target_pairs={{0,96},{32,0},{64,32},{96,64},{1,97},{33,1},{65,33},{97,65},{2,98}... | collective-permute-start | bytes 393224 | tf_op jit(solution)/shard_map/ppermute | solution.py:32
  147.5 1.2 collective-permute-done.5
  148.7 2.7 %collective-permute-done.7 = bf16[8,32,256]{2,1,0:T(8,128)(2,1)S(1)} collective-permute-done((bf16[8,32,256]{2,1,0:T(8,128)(2,1)S(1)}, bf16[8,32,256]{2,1,0:T(8,128)(2,1)S(1)}, u32[]{:S(2)}, u32[]{:S(2)}) %collective-permute-start.7) | collective-permute-done | bytes 131104 | tf_op jit(solution)/shard_map/ppermute | solution.py:32
  151.4 2.8 %all-to-all-done.4 = bf16[16,16,1152]{2,1,0:T(8,128)(2,1)S(1)} async-done(((bf16[16,16,1152]{2,1,0:T(8,128)(2,1)}), bf16[16,16,1152]{2,1,0:T(8,128)(2,1)S(1)}, u32[]{:S(2)}, u32[]{:S(2)}) %all-to-all-start.4) | async-done | bytes 589856 | tf_op jit(solution)/shard_map/all_to_all | solution.py:27
  155.0 50.5 %all_to_all.31.got_ref = bf16[8,72,256]{2,1,0:T(8,128)(2,1)S(1)} all-to-all(bf16[8,72,256]{2,1,0:T(8,128)(2,1)S(1)} %pad_maximum_fusion), channel_id=1, replica_groups=mesh['za'=2,'zb'=4,'x'=4,'c'=2,'zh'=4,'y'=4] {'za','zh'}, dimensions={0} | all-to-all | bytes 589824 | tf_op jit(solution)/shard_map/all_to_all | solution.py:27
  (40 shorter events, 10.0 us)
Async XLA Ops:
  2.4 66.6 %all-to-all-start = ((bf16[8,64,256]{2,1,0:T(8,128)(2,1)}), bf16[8,64,256]{2,1,0:T(8,128)(2,1)S(1)}, u32[]{:S(2)}, u32[]{:S(2)}) async-start(bf16[8,64,256]{2,1,0:T(8,128)(2,1)} %pack.1), calls=%async_computation | async-start | bytes 524288 | tf_op jit(solution)/shard_map/all_to_all | solution.py:27
  30.7 22.4 %collective-permute-start = (s32[16,5]{1,0:T(8,128)S(1)}, s32[16,5]{1,0:T(8,128)S(1)}, u32[]{:S(2)}, u32[]{:S(2)}) collective-permute-start(s32[16,5]{1,0:T(8,128)S(1)} %copy.32), channel_id=1, source_target_pairs={{0,512},{512,0},{1,513},{513,1},{2,514},{514,2},{3,515},{515,3},{4... | collective-permute-start | bytes 968 | tf_op jit(solution)/shard_map/ppermute | solution.py:32
  70.0 20.9 %all-to-all-start.1 = ((bf16[16,16,1024]{2,1,0:T(8,128)(2,1)}), bf16[16,16,1024]{2,1,0:T(8,128)(2,1)S(1)}, u32[]{:S(2)}, u32[]{:S(2)}) async-start(bf16[16,16,1024]{2,1,0:T(8,128)(2,1)} %bitcast.4), calls=%async_computation.1 | async-start | bytes 1048576 | tf_op jit(solution)/shard_map/all_to_all | solution.py:27
  76.0 11.4 %collective-permute-start.1 = (bf16[8,32,256]{2,1,0:T(8,128)(2,1)S(1)}, bf16[8,32,256]{2,1,0:T(8,128)(2,1)S(1)}, u32[]{:S(2)}, u32[]{:S(2)}) collective-permute-start(bf16[8,32,256]{2,1,0:T(8,128)(2,1)S(1)} %get-tuple-element.24.refs_0_), channel_id=1, source_target_pairs={{0,32},{32,64},{64,96},{96,0},{1,33},{33,65},{65,97},{97,1},{2,34}... | collective-permute-start | bytes 393224 | tf_op jit(solution)/shard_map/ppermute | solution.py:32
  79.4 8.4 %collective-permute-start.2 = (bf16[8,32,256]{2,1,0:T(8,128)(2,1)S(1)}, bf16[8,32,256]{2,1,0:T(8,128)(2,1)S(1)}, u32[]{:S(2)}, u32[]{:S(2)}) collective-permute-start(bf16[8,32,256]{2,1,0:T(8,128)(2,1)S(1)} %get-tuple-element.24.refs_0_), channel_id=1, source_target_pairs={{0,64},{32,96},{64,0},{96,32},{1,65},{33,97},{65,1},{97,33},{2,66}... | collective-permute-start | bytes 393224 | tf_op jit(solution)/shard_map/ppermute | solution.py:32
  84.0 6.9 %collective-permute-start.3 = (bf16[8,32,256]{2,1,0:T(8,128)(2,1)S(1)}, bf16[8,32,256]{2,1,0:T(8,128)(2,1)S(1)}, u32[]{:S(2)}, u32[]{:S(2)}) collective-permute-start(bf16[8,32,256]{2,1,0:T(8,128)(2,1)S(1)} %get-tuple-element.24.refs_0_), channel_id=1, source_target_pairs={{0,96},{32,0},{64,32},{96,64},{1,97},{33,1},{65,33},{97,65},{2,98}... | collective-permute-start | bytes 393224 | tf_op jit(solution)/shard_map/ppermute | solution.py:32
  90.9 3.8 %collective-permute-start.4 = (bf16[256,1024]{1,0:T(8,128)(2,1)S(1)}, bf16[256,1024]{1,0:T(8,128)(2,1)S(1)}, u32[]{:S(2)}, u32[]{:S(2)}) collective-permute-start(bf16[256,1024]{1,0:T(8,128)(2,1)S(1)} %bitcast.24), channel_id=1, source_target_pairs={{0,16},{16,0},{1,17},{17,1},{2,18},{18,2},{3,19},{19,3},{4,20},{20... | collective-permute-start | bytes 1572872 | tf_op jit(solution)/shard_map/ppermute | solution.py:32
  95.8 18.2 %all-to-all-start.2 = ((f32[16,16,512]{2,1,0:T(8,128)}), f32[16,16,512]{2,1,0:T(8,128)S(1)}, u32[]{:S(2)}, u32[]{:S(2)}) async-start(f32[16,16,512]{2,1,0:T(8,128)} %bitcast.6), calls=%async_computation.2 | async-start | bytes 1048576 | tf_op jit(solution)/shard_map/all_to_all | solution.py:27
  126.9 3.8 %collective-permute-start.8 = (bf16[256,1024]{1,0:T(8,128)(2,1)S(1)}, bf16[256,1024]{1,0:T(8,128)(2,1)S(1)}, u32[]{:S(2)}, u32[]{:S(2)}) collective-permute-start(bf16[256,1024]{1,0:T(8,128)(2,1)S(1)} %away.1), channel_id=1, source_target_pairs={{0,16},{16,0},{1,17},{17,1},{2,18},{18,2},{3,19},{19,3},{4,20},{20... | collective-permute-start | bytes 1572872 | tf_op jit(solution)/shard_map/ppermute | solution.py:32
  131.7 22.6 %all-to-all-start.4 = ((bf16[16,16,1152]{2,1,0:T(8,128)(2,1)}), bf16[16,16,1152]{2,1,0:T(8,128)(2,1)S(1)}, u32[]{:S(2)}, u32[]{:S(2)}) async-start(bf16[16,16,1152]{2,1,0:T(8,128)(2,1)} %bitcast.12), calls=%async_computation.4 | async-start | bytes 1179648 | tf_op jit(solution)/shard_map/all_to_all | solution.py:27
  137.8 11.0 %collective-permute-start.5 = (bf16[8,32,256]{2,1,0:T(8,128)(2,1)S(1)}, bf16[8,32,256]{2,1,0:T(8,128)(2,1)S(1)}, u32[]{:S(2)}, u32[]{:S(2)}) collective-permute-start(bf16[8,32,256]{2,1,0:T(8,128)(2,1)S(1)} %get-tuple-element.45), channel_id=1, source_target_pairs={{0,32},{32,64},{64,96},{96,0},{1,33},{33,65},{65,97},{97,1},{2,34}... | collective-permute-start | bytes 393224 | tf_op jit(solution)/shard_map/ppermute | solution.py:32
  140.1 8.6 %collective-permute-start.6 = (bf16[8,32,256]{2,1,0:T(8,128)(2,1)S(1)}, bf16[8,32,256]{2,1,0:T(8,128)(2,1)S(1)}, u32[]{:S(2)}, u32[]{:S(2)}) collective-permute-start(bf16[8,32,256]{2,1,0:T(8,128)(2,1)S(1)} %get-tuple-element.44), channel_id=1, source_target_pairs={{0,64},{32,96},{64,0},{96,32},{1,65},{33,97},{65,1},{97,33},{2,66}... | collective-permute-start | bytes 393224 | tf_op jit(solution)/shard_map/ppermute | solution.py:32
  144.1 7.4 %collective-permute-start.7 = (bf16[8,32,256]{2,1,0:T(8,128)(2,1)S(1)}, bf16[8,32,256]{2,1,0:T(8,128)(2,1)S(1)}, u32[]{:S(2)}, u32[]{:S(2)}) collective-permute-start(bf16[8,32,256]{2,1,0:T(8,128)(2,1)S(1)} %get-tuple-element.43), channel_id=1, source_target_pairs={{0,96},{32,0},{64,32},{96,64},{1,97},{33,1},{65,33},{97,65},{2,98}... | collective-permute-start | bytes 393224 | tf_op jit(solution)/shard_map/ppermute | solution.py:32
